TPU v7x, 128 devices: a whole 4x4x4 slice. The times are simulated.
128 devices in a mesh: store: 16 (over x, z), head: 8 (over y, core).
Axes of the slice: x: 4, y: 4, z: 4, core: 2. Of those that a mesh axis runs over, the one named last changes fastest.
Arguments:
- tile_inputs: bfloat16 [32, 256, 12288], P('store'), may hold values from -6 to 6
- tile_queries: bfloat16 [32, 256, 12288], P('store', 'head'), may hold values from -22 to 22
- key_weight: bfloat16 [12288, 1024], P('store', 'head'), may hold values from -0.0546875 to 0.0546875
- value_weight: bfloat16 [12288, 1024], P('store', 'head'), may hold values from -0.0546875 to 0.0546875
- span_keys: bfloat16 [256, 8, 512, 128], P('store', 'head'), may hold values from -6 to 6
- span_values: bfloat16 [256, 8, 512, 128], P('store', 'head'), may hold values from -6 to 6
- span_slot: int32 [256], replicated, may hold values from 0 to 255, as said below
- retrieval: int32 [32, 8], P('store'), may hold values from 0 to 255, as said below
- tile_ids: int32 [32, 2], P('store'), may hold values from 0 to 31, as said below
Outputs:
- attended: bfloat16 [32, 256, 12288], P('store', 'head')
Inputs may be any that keep to these rules, and one draw needn't show every extreme that they name: A permutation: span id c is held at row span_slot[c] of the store, on store device span_slot[c] // 16. `retrieval`: the 8 spans of one query lie on 8 different store devices. Among the spans named by the 2 queries of one store device, at most 1 lie on any one store device, and exactly 1 on some one. `tile_ids`: the 2 tiles of one query are distinct.
All inputs are finite; a program needn't handle non-finite values.
Results may differ from a plain program's by a relative error of at most 0.0068.
Values may be sent and summed in bfloat16 or wider, within the bound.
No kernel may reach another device: no remote copies, remote signals or barrier semaphores. Data moves between devices by JAX's collectives and lax.ppermute only.
A program may use at most 192 MiB of HBM per device.

v0:
```python
import jax
import jax.numpy as jnp
from jax import lax
from jax.sharding import PartitionSpec as P

rope_base = 1000000.0


def rotate(block_values, positions):
    half_width = block_values.shape[-1] // 2
    exponent = jnp.arange(half_width, dtype=jnp.float32) * (2.0 / block_values.shape[-1])
    frequency = jnp.power(jnp.float32(rope_base), -exponent)
    angle = positions.astype(jnp.float32)[..., None] * frequency
    cosine = jnp.cos(angle)
    sine = jnp.sin(angle)
    leading = block_values[..., :half_width]
    trailing = block_values[..., half_width:]
    return jnp.concatenate(
        [leading * cosine - trailing * sine, trailing * cosine + leading * sine], axis=-1
    )


def tile_positions(tile_list, tile_len):
    offsets = jnp.arange(tile_len, dtype=jnp.int32)
    return (tile_list[:, None] * tile_len + offsets[None, :]).reshape(-1)


def order_in_owner(owner_flat):
    count = owner_flat.shape[-1]
    same = owner_flat[:, None] == owner_flat[None, :]
    earlier = (
        jnp.arange(count, dtype=jnp.int32)[None, :] < jnp.arange(count, dtype=jnp.int32)[:, None]
    )
    return jnp.sum((same & earlier).astype(jnp.int32), axis=1)


def request_table(owner_flat, local_flat, owner_index, capacity):
    ranking = order_in_owner(owner_flat)
    owner_hit = owner_flat[None, None, :] == owner_index[:, None, None]
    rank_hit = ranking[None, None, :] == jnp.arange(capacity, dtype=jnp.int32)[None, :, None]
    chosen = jnp.where(owner_hit & rank_hit, local_flat[None, None, :] + 1, 0)
    return jnp.sum(chosen, axis=2) - 1


def body(
    tile_inputs,
    tile_queries,
    key_weight,
    value_weight,
    span_keys,
    span_values,
    span_slot,
    retrieval,
    tile_ids,
):
    queries_dev, tile_rows, width = tile_inputs.shape
    per_store = span_keys.shape[0]
    kv_local = span_keys.shape[1]
    span_len = span_keys.shape[2]
    head_dim = span_keys.shape[3]
    slot_count = retrieval.shape[1]
    recompute = tile_ids.shape[1]
    tile_len = tile_rows // recompute
    store_count = lax.axis_size("store")
    score_scale = head_dim ** (-0.5)
    flat_inputs = tile_inputs.reshape(queries_dev * tile_rows, width)
    fresh_keys = jnp.dot(
        flat_inputs,
        lax.all_gather(key_weight, "store", axis=0, tiled=True),
        preferred_element_type=jnp.float32,
    )
    fresh_values = jnp.dot(
        flat_inputs,
        lax.all_gather(value_weight, "store", axis=0, tiled=True),
        preferred_element_type=jnp.float32,
    )
    store_rows = span_slot[retrieval]
    owners = store_rows // per_store
    ranks = order_in_owner(owners.reshape(-1)).reshape(queries_dev, slot_count)
    local_rows = store_rows % per_store
    wanted = request_table(
        owners.reshape(-1),
        local_rows.reshape(-1),
        jnp.arange(store_count, dtype=jnp.int32),
        queries_dev,
    )
    incoming = lax.all_to_all(wanted, "store", split_axis=0, concat_axis=0, tiled=True)
    picked = jnp.clip(incoming, 0, per_store - 1).reshape(-1)
    present = (incoming >= 0).reshape(-1)[:, None, None, None]
    block_shape = (store_count, queries_dev, kv_local, span_len, head_dim)
    send_keys = jnp.where(present, span_keys[picked], jnp.zeros((), span_keys.dtype)).reshape(
        block_shape
    )
    send_values = jnp.where(present, span_values[picked], jnp.zeros((), span_values.dtype)).reshape(
        block_shape
    )
    got_keys, got_values = (
        lax.all_to_all(send_keys, "store", split_axis=0, concat_axis=0, tiled=True),
        lax.all_to_all(send_values, "store", split_axis=0, concat_axis=0, tiled=True),
    )
    head_queries = lax.all_to_all(tile_queries, "head", split_axis=2, concat_axis=1, tiled=True)
    offsets = (jnp.arange(slot_count, dtype=jnp.int32) * span_len)[:, None, None]
    key_positions = jnp.arange(slot_count * span_len, dtype=jnp.int32)
    fresh_key_rows = fresh_keys.reshape(queries_dev, tile_rows, kv_local, head_dim)
    fresh_value_rows = fresh_values.astype(jnp.bfloat16).reshape(
        queries_dev, tile_rows, kv_local, head_dim
    )
    anchor = jnp.zeros((), jnp.int32)
    results = []
    for query_number in range(queries_dev):
        owner_row = owners[query_number]
        rank_row = ranks[query_number]
        stored_keys = rotate(got_keys[owner_row, rank_row].astype(jnp.float32), offsets).astype(
            jnp.bfloat16
        )
        key_block = stored_keys.transpose(1, 0, 2, 3).reshape(
            kv_local, slot_count * span_len, head_dim
        )
        value_block = (
            got_values[owner_row, rank_row]
            .transpose(1, 0, 2, 3)
            .reshape(kv_local, slot_count * span_len, head_dim)
        )
        positions = tile_positions(tile_ids[query_number], tile_len)
        new_keys = (
            rotate(fresh_key_rows[query_number], positions[:, None])
            .astype(jnp.bfloat16)
            .transpose(1, 0, 2)
        )
        new_values = fresh_value_rows[query_number].transpose(1, 0, 2)
        for tile_number in range(recompute):
            start = tile_ids[query_number, tile_number] * tile_len
            lower = tile_number * tile_len
            key_block = lax.dynamic_update_slice(
                key_block, new_keys[:, lower : lower + tile_len], (anchor, start, anchor)
            )
            value_block = lax.dynamic_update_slice(
                value_block, new_values[:, lower : lower + tile_len], (anchor, start, anchor)
            )
        grouped = head_queries[query_number].reshape(tile_rows, kv_local, -1, head_dim)
        scores = (
            jnp.einsum("rkgd,ksd->kgrs", grouped, key_block, preferred_element_type=jnp.float32)
            * score_scale
        )
        allowed = key_positions[None, :] <= positions[:, None]
        scores = jnp.where(allowed[None, None], scores, -1e30)
        row_max = jnp.max(scores, axis=-1, keepdims=True)
        weights = jnp.exp(scores - row_max)
        row_total = jnp.sum(weights, axis=-1)
        rounded = weights.astype(jnp.bfloat16)
        mixed_sum = jnp.einsum(
            "kgrs,ksd->rkgd", rounded, value_block, preferred_element_type=jnp.float32
        )
        normed = mixed_sum / row_total.transpose(2, 0, 1)[..., None]
        results.append(normed.astype(jnp.bfloat16).reshape(tile_rows, -1))
    stacked = jnp.stack(results)
    return lax.all_to_all(stacked, "head", split_axis=1, concat_axis=2, tiled=True)


def solution(mesh):
    placed = (
        P("store", None, None),
        P("store", "head", None),
        P("store", "head"),
        P("store", "head"),
        P("store", "head", None, None),
        P("store", "head", None, None),
        P(),
        P("store", None),
        P("store", None),
    )
    return jax.shard_map(
        body, mesh=mesh, in_specs=placed, out_specs=P("store", "head", None), check_vma=False
    )
```

profile of v0, /device:TPU:6, one launch (start us, length us, event | category | flops | bytes accessed | tf_op | source)
XLA Modules:
  0.0 395.9 jit_solution(18048689886692318978)
XLA Ops:
  10.4 8.3 %all-to-all-start = ((s32[16,1,2]{2,1,0:T(1,128)}), s32[16,1,2]{2,1,0:T(1,128)S(1)}, u32[]{:S(2)}, u32[]{:S(2)}) async-start(s32[16,1,2]{2,1,0:T(1,128)} %copy.87), calls=%async_computation | async-start | bytes 16384 | tf_op jit(solution)/shard_map/all_to_all | solution.py:87
  18.7 13.3 %copy.95 = bf16[2,32,12288]{1,0,2:T(2,128)(2,1)} copy(bf16[2,32,12288]{2,1,0:T(8,128)(2,1)} %param.10) | data formatting | bytes 3145728 | tf_op args[1]
  32.0 9.5 %reshape.1034 = bf16[8,2,49152]{2,1,0:T(2,128)(2,1)} reshape(bf16[12288,2,32]{2,1,0:T(2,128)(2,1)} %bitcast.195) | data formatting | bytes 3145728
  41.5 4.5 %all-to-all-start.3 = ((bf16[8,2,49152]{2,1,0:T(2,128)(2,1)}), bf16[8,2,49152]{2,1,0:T(2,128)(2,1)}, u32[]{:S(2)}, u32[]{:S(2)}) async-start(bf16[8,2,49152]{2,1,0:T(2,128)(2,1)} %reshape.1034), calls=%async_computation.3 | async-start | bytes 3145728 | tf_op jit(solution)/shard_map/all_to_all | solution.py:101
  46.3 3.0 gather_fusion.3
  49.4 4.7 %gather_fusion.1 = bf16[32,512,128]{2,1,0:T(8,128)(2,1)} fusion(bf16[16,512,128]{2,1,0:T(8,128)(2,1)} %bitcast.202, s32[1024]{0:T(1024)S(1)} %pad_clamp_fusion), kind=kCustom, calls=%fused_computation.1 | custom fusion | bytes 8388736 | tf_op jit(solution)/shard_map/gather | solution.py:94
  54.1 5.9 %broadcast_select_fusion.1 = (bf16[16,2,1,512,128]{4,3,1,2,0:T(8,128)(2,1)}, bf16[16,2,1,512,128]{4,3,1,2,0:T(8,128)(2,1)}) fusion(bf16[16,2,1,512,128]{4,3,1,2,0:T(8,128)(2,1)} %bitcast.197, pred[16,2]{1,0:T(8,128)(4,1)S(1)} %copy.89, bf16[16,2,1,512,128]{4,3,1,2,0:T(8,128)(2,1)} %bitcast.196), kind=kLoop, calls=%fused_computation.26 | loop fusion | flops 4194304 | bytes 16777248 | tf_op jit(solution)/shard_map/jit(_where)/select_n | solution.py:94
  60.0 7.7 %all-to-all-done.3 = bf16[8,2,49152]{2,1,0:T(2,128)(2,1)} async-done(((bf16[8,2,49152]{2,1,0:T(2,128)(2,1)}), bf16[8,2,49152]{2,1,0:T(2,128)(2,1)}, u32[]{:S(2)}, u32[]{:S(2)}) %all-to-all-start.3) | async-done | bytes 1572896 | tf_op jit(solution)/shard_map/all_to_all | solution.py:101
  67.7 55.9 %all_to_all.49 = bf16[16,2,1,512,128]{4,3,1,2,0:T(8,128)(2,1)} all-to-all(bf16[16,2,1,512,128]{4,3,1,2,0:T(8,128)(2,1)} %get-tuple-element.30), channel_id=1, replica_groups=mesh['store'=16,'head'=8] {'store'}, dimensions={0} | all-to-all | bytes 8388608 | tf_op jit(solution)/shard_map/all_to_all | solution.py:98
  123.6 6.6 %all-to-all-start.1 = ((bf16[16,2,1,512,128]{4,3,1,2,0:T(8,128)(2,1)}), bf16[16,2,1,512,128]{4,3,1,2,0:T(8,128)(2,1)}, u32[]{:S(2)}, u32[]{:S(2)}) async-start(bf16[16,2,1,512,128]{4,3,1,2,0:T(8,128)(2,1)} %get-tuple-element.29), calls=%async_computation.1 | async-start | bytes 8388608 | tf_op jit(solution)/shard_map/all_to_all | solution.py:99
  136.9 7.9 %reshape.1035 = bf16[12288,2,32]{2,1,0:T(2,128)(2,1)} reshape(bf16[8,2,49152]{2,1,0:T(2,128)(2,1)} %all-to-all-done.3) | data formatting | bytes 3145728
  144.8 13.4 %copy.96 = bf16[2,32,8,1536]{3,1,2,0:T(8,128)(2,1)S(1)} copy(bf16[2,32,8,1536]{1,0,3,2:T(2,128)(2,1)} %bitcast.194) | data formatting | bytes 3145728 | tf_op jit(solution)/shard_map/all_to_all | solution.py:101
  159.5 2.4 reshape.935
  161.9 2.4 reshape.942
  164.3 3.8 gather_fusion.6
  168.1 3.9 gather_fusion.4
  172.0 12.2 %all-to-all-done.1 = bf16[16,2,1,512,128]{4,3,1,2,0:T(8,128)(2,1)} async-done(((bf16[16,2,1,512,128]{4,3,1,2,0:T(8,128)(2,1)}), bf16[16,2,1,512,128]{4,3,1,2,0:T(8,128)(2,1)}, u32[]{:S(2)}, u32[]{:S(2)}) %all-to-all-start.1) | async-done | bytes 4194336 | tf_op jit(solution)/shard_map/all_to_all | solution.py:99
  184.3 2.9 gather_fusion.2
  187.2 2.9 gather_fusion.5
  192.8 1.8 bitcast_convert_fusion
  198.3 10.0 %fusion.79 = f32[512,128]{0,1:T(8,128)S(1)} fusion(bf16[512,12288]{1,0:T(8,128)(2,1)} %bitcast.198, bf16[12288,128]{1,0:T(8,128)(2,1)} %all-gather.5.cloned.1.call-done), kind=kOutput, calls=%fused_computation.159 | convolution fusion | flops 1610612736 | bytes 15990784 | tf_op jit(solution)/shard_map/dot_general | solution.py:67
  209.4 8.9 %convolution_convert_fusion = bf16[512,128]{1,0:T(8,128)(2,1)S(1)} fusion(bf16[512,12288]{1,0:T(8,128)(2,1)} %bitcast.199, bf16[12288,128]{1,0:T(8,128)(2,1)} %all-gather.3.cloned.1.call-done), kind=kOutput, calls=%fused_computation.36 | convolution fusion | flops 1610678272 | bytes 15859712 | tf_op jit(solution)/shard_map/dot_general | solution.py:72
  224.5 21.1 %fusion.5 = (f32[12,256]{1,0:T(8,128)S(1)}, f32[4096,256,12]{1,0,2:T(8,128)}) fusion(pred[256,4096]{0,1:T(8,128)(4,1)S(1)} %copy-done.2, bf16[256,12,128]{2,1,0:T(8,128)(2,1)} %reshape.942, bf16[4096,128]{1,0:T(8,128)(2,1)} %constant_dynamic-update-slice_fusion), kind=kOutput, calls=%fused_computation.16 | convolution fusion | flops 3258971136 | bytes 53227520 | tf_op jit(solution)/shard_map/rkgd,ksd->kgrs/dot_general | solution.py:142
  245.6 21.3 %fusion.2 = f32[12,256]{1,0:T(8,128)S(1)} fusion(f32[4096,256,12]{1,0,2:T(8,128)} %get-tuple-element.50, f32[12,256]{1,0:T(8,128)S(1)} %get-tuple-element.49, pred[256,4096]{0,1:T(8,128)(4,1)S(1)} %copy-done.2), kind=kLoop, calls=%fused_computation.13 | loop fusion | flops 50328576 | bytes 51404800 | tf_op jit(solution)/shard_map/reduce_sum | solution.py:149
  266.8 20.4 %fusion.14 = bf16[256,1,12,128]{0,3,2,1:T(8,128)(2,1)} fusion(f32[4096,256,12]{1,0,2:T(8,128)} %get-tuple-element.50, f32[12,256]{1,0:T(8,128)S(1)} %get-tuple-element.49, pred[256,4096]{0,1:T(8,128)(4,1)S(1)} %copy-done.2, bf16[4096,128]{0,1:T(8,128)(2,1)S(1)} %copy-done.4, f32[256,12]{0,1:T(8,128)S(1)} %bitcast.213), kind=kOutput, calls=%fused_computation.33 | convolution fusion | flops 3272343552 | bytes 53239808 | tf_op jit(solution)/shard_map/kgrs,ksd->rkgd/dot_general | solution.py:151
  287.2 4.8 %copy.107 = bf16[1,256,1536]{2,0,1:T(2,128)(2,1)} copy(bf16[1,256,1536]{1,2,0:T(8,128)(2,1)} %bitcast.211) | data formatting | bytes 1572864 | tf_op jit(solution)/shard_map/stack;reshape | solution.py:156
  293.3 19.7 %fusion.4 = (f32[12,256]{1,0:T(8,128)S(1)}, f32[4096,256,12]{1,0,2:T(8,128)}) fusion(pred[256,4096]{0,1:T(8,128)(4,1)S(1)} %iota_compare_fusion.1, bf16[256,12,128]{2,1,0:T(8,128)(2,1)} %reshape.935, bf16[4096,128]{1,0:T(8,128)(2,1)S(1)} %constant_dynamic-update-slice_fusion.4), kind=kOutput, calls=%fused_computation.15 | convolution fusion | flops 3258971136 | bytes 53227520 | tf_op jit(solution)/shard_map/rkgd,ksd->kgrs/dot_general | solution.py:142
  313.0 21.3 %fusion = f32[12,256]{1,0:T(8,128)S(1)} fusion(f32[4096,256,12]{1,0,2:T(8,128)} %get-tuple-element.52, f32[12,256]{1,0:T(8,128)S(1)} %get-tuple-element.51, pred[256,4096]{0,1:T(8,128)(4,1)S(1)} %iota_compare_fusion.1), kind=kLoop, calls=%fused_computation.11 | loop fusion | flops 50328576 | bytes 51404800 | tf_op jit(solution)/shard_map/reduce_sum | solution.py:149
  334.3 19.7 %fusion.15 = bf16[256,1,12,128]{0,3,2,1:T(8,128)(2,1)S(1)} fusion(f32[4096,256,12]{1,0,2:T(8,128)} %get-tuple-element.52, f32[12,256]{1,0:T(8,128)S(1)} %get-tuple-element.51, pred[256,4096]{0,1:T(8,128)(4,1)S(1)} %iota_compare_fusion.1, bf16[4096,128]{0,1:T(8,128)(2,1)S(1)} %copy-done.3, f32[256,12]{0,1:T(8,128)S(1)} %bitcast.214), kind=kOutput, calls=%fused_computation.35 | convolution fusion | flops 3272343552 | bytes 53239808 | tf_op jit(solution)/shard_map/kgrs,ksd->rkgd/dot_general | solution.py:151
  354.0 3.0 copy.106
  357.0 4.7 %pad_maximum_fusion = bf16[2,256,1536]{2,0,1:T(2,128)(2,1)S(1)} fusion(bf16[1,256,1536]{2,0,1:T(2,128)(2,1)} %copy.107, bf16[1,256,1536]{2,0,1:T(2,128)(2,1)} %copy.106), kind=kLoop, calls=%fused_computation.31 | loop fusion | flops 3145728 | bytes 3145728 | tf_op jit(solution)/shard_map/stack | solution.py:156
  361.8 25.9 %all_to_all.50 = bf16[2,256,1536]{2,0,1:T(2,128)(2,1)S(1)} all-to-all(bf16[2,256,1536]{2,0,1:T(2,128)(2,1)S(1)} %pad_maximum_fusion), channel_id=1, replica_groups=mesh['store'=16,'head'=8] {'head'}, dimensions={1} | all-to-all | bytes 3145728 | tf_op jit(solution)/shard_map/all_to_all | solution.py:157
  (78 shorter events, 25.8 us)
Async XLA Ops:
  6.5 39.8 %copy-start = (bf16[16,1,512,128]{3,2,1,0:T(8,128)(2,1)S(1)}, bf16[16,1,512,128]{3,2,1,0:T(8,128)(2,1)}, u32[]{:S(2)}) copy-start(bf16[16,1,512,128]{3,2,1,0:T(8,128)(2,1)} %param.13) | copy-start | bytes 6291460
  6.5 191.8 %all-gather.5.cloned.1.call-start = ((), (), s32[]{:S(2)}) async-start(), calls=%async_computation.6 | async-start | bytes 3342336 | tf_op jit(solution)/shard_map/all_gather | solution.py:69
  10.4 31.1 %all-to-all-start = ((s32[16,1,2]{2,1,0:T(1,128)}), s32[16,1,2]{2,1,0:T(1,128)S(1)}, u32[]{:S(2)}, u32[]{:S(2)}) async-start(s32[16,1,2]{2,1,0:T(1,128)} %copy.87), calls=%async_computation | async-start | bytes 16384 | tf_op jit(solution)/shard_map/all_to_all | solution.py:87
  41.5 26.1 %all-to-all-start.3 = ((bf16[8,2,49152]{2,1,0:T(2,128)(2,1)}), bf16[8,2,49152]{2,1,0:T(2,128)(2,1)}, u32[]{:S(2)}, u32[]{:S(2)}) async-start(bf16[8,2,49152]{2,1,0:T(2,128)(2,1)} %reshape.1034), calls=%async_computation.3 | async-start | bytes 3145728 | tf_op jit(solution)/shard_map/all_to_all | solution.py:101
  123.6 7.4 %copy-start.5 = (s32[2,2]{1,0:T(2,128)S(1)}, s32[2,2]{1,0:T(2,128)}, u32[]{:S(2)}) copy-start(s32[2,2]{1,0:T(2,128)} %param.17) | copy-start | bytes 52
  123.6 60.7 %all-to-all-start.1 = ((bf16[16,2,1,512,128]{4,3,1,2,0:T(8,128)(2,1)}), bf16[16,2,1,512,128]{4,3,1,2,0:T(8,128)(2,1)}, u32[]{:S(2)}, u32[]{:S(2)}) async-start(bf16[16,2,1,512,128]{4,3,1,2,0:T(8,128)(2,1)} %get-tuple-element.29), calls=%async_computation.1 | async-start | bytes 8388608 | tf_op jit(solution)/shard_map/all_to_all | solution.py:99
  130.2 79.2 %all-gather.3.cloned.1.call-start = ((), (), s32[]{:S(2)}) async-start(), calls=%async_computation.5 | async-start | bytes 3342336 | tf_op jit(solution)/shard_map/all_gather | solution.py:74
  208.3 16.1 %copy-start.2 = (pred[256,4096]{0,1:T(8,128)(4,1)S(1)}, pred[256,4096]{0,1:T(8,128)(4,1)}, u32[]{:S(2)}) copy-start(pred[256,4096]{0,1:T(8,128)(4,1)} %iota_compare_fusion) | copy-start | bytes 3145732
  245.6 21.3 %copy-start.4 = (bf16[4096,128]{0,1:T(8,128)(2,1)S(1)}, bf16[4096,128]{0,1:T(8,128)(2,1)}, u32[]{:S(2)}) copy-start(bf16[4096,128]{0,1:T(8,128)(2,1)} %constant_dynamic-update-slice_fusion.2) | copy-start | bytes 3145732
  313.0 21.3 %copy-start.3 = (bf16[4096,128]{0,1:T(8,128)(2,1)S(1)}, bf16[4096,128]{0,1:T(8,128)(2,1)}, u32[]{:S(2)}) copy-start(bf16[4096,128]{0,1:T(8,128)(2,1)} %constant_dynamic-update-slice_fusion.6) | copy-start | bytes 3145732
  357.0 32.1 %copy-start.1 = (bf16[16,1,512,128]{3,2,1,0:T(8,128)(2,1)S(1)}, bf16[16,1,512,128]{3,2,1,0:T(8,128)(2,1)}, u32[]{:S(2)}) copy-start(bf16[16,1,512,128]{3,2,1,0:T(8,128)(2,1)} %param.13) | copy-start | bytes 6291460
Sparse Core Ops, SparseCore 0:
  9.5 49.6 all-gather.4
  133.2 76.1 all-gather.2
where the time goes:
time: 400 us; the launch traced here: 396 us
  matrix products  99.9 us (25%)
  local copies, waits for them, and re-layouts  93.3 us (23%)
  blocking collectives  81.8 us (20%)
  other arithmetic  62.9 us (16%)
  waiting for transfers between devices  22.4 us (6%)
  starting transfers between devices  19.4 us (5%)
  between operations  16.2 us (4%)
    all_to_all x1, blocking collectives, body(): lax.all_to_all(send_keys, 'store', split_axis=0, concat_axis=0, tiled=True)  55.9 us
    reduce_sum x2, other arithmetic, body(): row_total = jnp.sum(weights, axis=-1)  42.5 us
    dot_general x2, matrix products, body(): jnp.einsum('rkgd,ksd->kgrs', grouped, key_block, preferred_element_type=j...  40.8 us
    dot_general x2, matrix products, body(): jnp.einsum('kgrs,ksd->rkgd', rounded, value_block, preferred_element_type...  40.2 us
    unnamed x15, local copies, waits for them, and re-layouts  30.8 us
    all_to_all x1, blocking collectives, body(): lax.all_to_all(stacked, 'head', split_axis=1, concat_axis=2, tiled=True)  25.9 us
    all_to_all x1, local copies, waits for them, and re-layouts, body(): lax.all_to_all(tile_queries, 'head', split_axis=2, concat_axis=1, tiled=T...  13.4 us
    all_to_all x1, waiting for transfers between devices, body(): lax.all_to_all(send_values, 'store', split_axis=0, concat_axis=0, tiled=T...  12.2 us
  transfers between devices with their start and end apart: 5, of which 3 were waited for; matrix products, arithmetic and copies ran while one was open for 26% of the time, Pallas kernels for 0%

commit v1 on v0

v1 whole, which is shorter than its diff:
```python
import functools
import math

import jax
import jax.numpy as jnp
from jax import lax
from jax.experimental import pallas as pl
from jax.experimental.pallas import tpu as pltpu
from jax.sharding import PartitionSpec as P

rope_base = 1000000.0
low = -1e30


def rope_tables(positions, width):
    half_width = width // 2
    exponent = jnp.arange(half_width, dtype=jnp.float32) * (2.0 / width)
    frequency = jnp.power(jnp.float32(rope_base), -exponent)
    angle = positions.astype(jnp.float32)[..., None] * frequency
    cosine = jnp.cos(angle)
    sine = jnp.sin(angle)
    return (
        jnp.concatenate([cosine, cosine], axis=-1),
        jnp.concatenate([-sine, sine], axis=-1),
    )


def rotate(values, cosine, signed_sine):
    swapped = pltpu.roll(values, values.shape[-1] // 2, 1)
    return values * cosine + swapped * signed_sine


def whole(shape):
    return pl.BlockSpec(shape, lambda *_: (0,) * len(shape))


def split_kernel(x_ref, o_ref):
    o_ref[0] = x_ref[...]


def split_columns(x, pieces):
    lead, rows, width = x.shape
    part = width // pieces
    return pl.pallas_call(
        split_kernel,
        grid=(pieces,),
        in_specs=[pl.BlockSpec((lead, rows, part), lambda j: (0, 0, j))],
        out_specs=pl.BlockSpec((1, lead, rows, part), lambda j: (j, 0, 0, 0)),
        out_shape=jax.ShapeDtypeStruct((pieces, lead, rows, part), x.dtype),
        name="split_columns",
    )(x)


def join_kernel(x_ref, o_ref):
    o_ref[...] = x_ref[0]


def join_columns(x):
    pieces, lead, rows, part = x.shape
    return pl.pallas_call(
        join_kernel,
        grid=(pieces,),
        in_specs=[pl.BlockSpec((1, lead, rows, part), lambda j: (j, 0, 0, 0))],
        out_specs=pl.BlockSpec((lead, rows, part), lambda j: (0, 0, j)),
        out_shape=jax.ShapeDtypeStruct((lead, rows, pieces * part), x.dtype),
        name="join_columns",
    )(x)


def pick_kernel(rows_ref, keys_ref, values_ref, o_ref, sems):
    count = o_ref.shape[0]
    copies = []
    for d in range(count):
        row = rows_ref[d]
        copies.append(pltpu.make_async_copy(keys_ref.at[row, 0], o_ref.at[d, 0], sems.at[d, 0]))
        copies.append(pltpu.make_async_copy(values_ref.at[row, 0], o_ref.at[d, 1], sems.at[d, 1]))
    for copy in copies:
        copy.start()
    for copy in copies:
        copy.wait()


def pick_spans(rows, keys, values):
    count = rows.shape[0]
    span_len, head_dim = keys.shape[2:]
    return pl.pallas_call(
        pick_kernel,
        in_specs=[
            pl.BlockSpec(memory_space=pltpu.SMEM),
            pl.BlockSpec(memory_space=pl.ANY),
            pl.BlockSpec(memory_space=pl.ANY),
        ],
        out_specs=pl.BlockSpec(memory_space=pl.ANY),
        out_shape=jax.ShapeDtypeStruct((count, 2, span_len, head_dim), keys.dtype),
        scratch_shapes=[pltpu.SemaphoreType.DMA((count, 2))],
        name="pick_spans",
    )(rows, keys, values)


def head_rows(q_ref, head_dim):
    tile = q_ref[...].reshape(-1, q_ref.shape[-1])
    heads = tile.shape[-1] // head_dim
    return [tile[:, g * head_dim : (g + 1) * head_dim] for g in range(heads)]


def stored_kernel(
    exp_scale, owner_ref, tile_ref, q_ref, got_ref, cos_ref, sin_ref, acc_ref, stat_ref, q_all, m_all, acc_all
):
    query = pl.program_id(0)
    number = pl.program_id(1)
    span_len, head_dim = got_ref.shape[2:]
    own = tile_ref[query, number]
    other = tile_ref[query, 1 - number]
    tile_len = q_ref.shape[0] * q_ref.shape[2]
    pair = 2 * tile_len
    per_span = span_len // tile_len
    lane = lax.broadcasted_iota(jnp.int32, (tile_len, head_dim), 1)
    marker = (lane == 0).astype(jnp.bfloat16)
    for g, part in enumerate(head_rows(q_ref, head_dim)):
        q_all[g * tile_len : (g + 1) * tile_len, :head_dim] = part
        q_all[g * tile_len : (g + 1) * tile_len, head_dim:] = marker
    m_all[...] = jnp.full_like(m_all, low)
    acc_all[...] = jnp.zeros_like(acc_all)
    key_lane = lax.broadcasted_iota(jnp.int32, (span_len, head_dim), 1)
    key_row = lax.broadcasted_iota(jnp.int32, (span_len, head_dim), 0)
    ones = jnp.ones((span_len, head_dim), jnp.bfloat16)

    def step(p, carry):
        owner = owner_ref[query, p]
        keys = rotate(
            got_ref[owner, 0].astype(jnp.float32), cos_ref[pl.ds(p, 1), :], sin_ref[pl.ds(p, 1), :]
        ).astype(jnp.bfloat16)
        key_tile = p * per_span + key_row // tile_len
        hidden = (key_lane == 0) & ((key_tile >= own) | (key_tile == other))
        keys = jnp.concatenate([keys, jnp.where(hidden, low, 0.0).astype(jnp.bfloat16)], axis=1)
        values = jnp.concatenate([got_ref[owner, 1], ones], axis=1)
        for start in range(0, q_all.shape[0], pair):
            at = pl.ds(start, pair)
            scores = lax.dot_general(
                q_all[at, :], keys, (((1,), (1,)), ((), ())), preferred_element_type=jnp.float32
            )
            before = m_all[at, :]
            after = jnp.maximum(before, jnp.max(scores, axis=1, keepdims=True))
            weights = jnp.exp2((scores - after[:, :1]) * exp_scale)
            fade = jnp.exp2((before - after) * exp_scale)
            acc_all[at, :] = acc_all[at, :] * fade[:, :1] + jnp.dot(
                weights.astype(jnp.bfloat16), values, preferred_element_type=jnp.float32
            )
            m_all[at, :] = after
        return carry

    lax.fori_loop(0, (own + per_span - 1) // per_span, step, 0)
    acc_ref[0, 0] = acc_all[:, :head_dim]
    wide = lax.broadcasted_iota(jnp.int32, m_all.shape, 1)
    stat_ref[0, 0] = jnp.where(wide < head_dim // 2, m_all[...], acc_all[:, head_dim:])


def stored_attention(owner, tile_ids, queries, got, cosine, signed_sine, exp_scale):
    sources, queries_dev, rows, part = queries.shape
    recompute = tile_ids.shape[1]
    head_dim = got.shape[3]
    per_tile = sources // recompute
    tile_len = per_tile * rows
    all_rows = tile_len * (part // head_dim)
    state = jax.ShapeDtypeStruct((queries_dev, recompute, all_rows, head_dim), jnp.float32)
    state_spec = pl.BlockSpec((1, 1, all_rows, head_dim), lambda i, j, *_: (i, j, 0, 0))
    return pl.pallas_call(
        functools.partial(stored_kernel, exp_scale),
        grid_spec=pltpu.PrefetchScalarGridSpec(
            num_scalar_prefetch=2,
            grid=(queries_dev, recompute),
            in_specs=[
                pl.BlockSpec((per_tile, 1, rows, part), lambda i, j, *_: (j, i, 0, 0)),
                whole(got.shape),
                whole(cosine.shape),
                whole(signed_sine.shape),
            ],
            out_specs=[state_spec, state_spec],
            scratch_shapes=[
                pltpu.VMEM((all_rows, 2 * head_dim), jnp.bfloat16),
                pltpu.VMEM((all_rows, head_dim), jnp.float32),
                pltpu.VMEM((all_rows, 2 * head_dim), jnp.float32),
            ],
        ),
        out_shape=[state, state],
        compiler_params=pltpu.CompilerParams(vmem_limit_bytes=48 * 2**20),
        cost_estimate=pl.CostEstimate(
            flops=8 * 10**9, bytes_accessed=15 * 10**6, transcendentals=16 * 10**6
        ),
        name="stored_attention",
    )(owner, tile_ids, queries, got, cosine, signed_sine)


def project_kernel(x_ref, w_ref, cos_ref, sin_ref, keys_ref, values_ref, total):
    step = pl.program_id(0)
    head_dim = keys_ref.shape[1]

    @pl.when(step == 0)
    def _():
        total[...] = jnp.zeros_like(total)

    total[...] += jnp.dot(x_ref[...], w_ref[...], preferred_element_type=jnp.float32)

    @pl.when(step == pl.num_programs(0) - 1)
    def _():
        keys_ref[...] = rotate(total[:, :head_dim], cos_ref[...], sin_ref[...]).astype(jnp.bfloat16)
        values_ref[...] = total[:, head_dim:].astype(jnp.bfloat16)


def project(x, weights, cosine, signed_sine):
    rows, width = x.shape
    columns = weights.shape[1]
    head_dim = columns // 2
    depth = 1536
    out = jax.ShapeDtypeStruct((rows, head_dim), jnp.bfloat16)
    return pl.pallas_call(
        project_kernel,
        grid=(width // depth,),
        in_specs=[
            pl.BlockSpec((rows, depth), lambda k: (0, k)),
            pl.BlockSpec((depth, columns), lambda k: (k, 0)),
            whole(cosine.shape),
            whole(signed_sine.shape),
        ],
        out_specs=[whole(out.shape), whole(out.shape)],
        out_shape=[out, out],
        scratch_shapes=[pltpu.VMEM((rows, columns), jnp.float32)],
        compiler_params=pltpu.CompilerParams(vmem_limit_bytes=48 * 2**20),
        cost_estimate=pl.CostEstimate(
            flops=2 * rows * width * columns, bytes_accessed=2 * width * (rows + columns), transcendentals=0
        ),
        name="project",
    )(x, weights, cosine, signed_sine)


def fresh_kernel(exp_scale, tile_ref, q_ref, keys_ref, values_ref, acc_ref, stat_ref, o_ref):
    query = pl.program_id(0)
    number = pl.program_id(1)
    rows, head_dim = keys_ref.shape
    tile_len = rows // 2
    own = tile_ref[query, number]
    other = tile_ref[query, 1 - number]
    row = lax.broadcasted_iota(jnp.int32, (tile_len, rows), 0)
    column = lax.broadcasted_iota(jnp.int32, (tile_len, rows), 1)
    in_own = column // tile_len == number
    allowed = (in_own & (column % tile_len <= row)) | (jnp.logical_not(in_own) & (other < own))
    bias = jnp.where(allowed, 0.0, low)
    keys = keys_ref[...]
    values = jnp.concatenate([values_ref[...], jnp.ones((rows, head_dim), jnp.bfloat16)], axis=1)
    half = head_dim // 2
    for g, part in enumerate(head_rows(q_ref, head_dim)):
        at = pl.ds(g * tile_len, tile_len)
        scores = lax.dot_general(
            part, keys, (((1,), (1,)), ((), ())), preferred_element_type=jnp.float32
        )
        scores = scores + bias
        stat = stat_ref[0, 0, at, :]
        before = stat[:, :1]
        after = jnp.maximum(before, jnp.max(scores, axis=1, keepdims=True))
        weights = jnp.exp2((scores - after) * exp_scale)
        fade = jnp.exp2((before - after) * exp_scale)
        mixed = jnp.dot(weights.astype(jnp.bfloat16), values, preferred_element_type=jnp.float32)
        total = stat[:, half : half + 1] * fade + mixed[:, head_dim : head_dim + 1]
        result = (acc_ref[0, 0, at, :] * fade + mixed[:, :head_dim]) / total
        o_ref[:, 0, :, g * head_dim : (g + 1) * head_dim] = result.astype(jnp.bfloat16).reshape(
            o_ref.shape[0], o_ref.shape[2], head_dim
        )


def fresh_attention(tile_ids, queries, keys, values, acc, stat, exp_scale):
    sources, queries_dev, rows, part = queries.shape
    recompute = tile_ids.shape[1]
    head_dim = keys.shape[1]
    per_tile = sources // recompute
    tile_rows = keys.shape[0] // queries_dev
    q_spec = pl.BlockSpec((per_tile, 1, rows, part), lambda i, j, *_: (j, i, 0, 0))
    key_spec = pl.BlockSpec((tile_rows, head_dim), lambda i, j, *_: (i, 0))
    state_spec = pl.BlockSpec((1, 1) + acc.shape[2:], lambda i, j, *_: (i, j, 0, 0))
    return pl.pallas_call(
        functools.partial(fresh_kernel, exp_scale),
        grid_spec=pltpu.PrefetchScalarGridSpec(
            num_scalar_prefetch=1,
            grid=(queries_dev, recompute),
            in_specs=[q_spec, key_spec, key_spec, state_spec, state_spec],
            out_specs=q_spec,
        ),
        out_shape=jax.ShapeDtypeStruct(queries.shape, queries.dtype),
        compiler_params=pltpu.CompilerParams(vmem_limit_bytes=48 * 2**20),
        cost_estimate=pl.CostEstimate(
            flops=10**9, bytes_accessed=10 * 10**6, transcendentals=2 * 10**6
        ),
        name="fresh_attention",
    )(tile_ids, queries, keys, values, acc, stat)


def body(
    tile_inputs,
    tile_queries,
    key_weight,
    value_weight,
    span_keys,
    span_values,
    span_slot,
    retrieval,
    tile_ids,
):
    queries_dev, tile_rows, width = tile_inputs.shape
    per_store, _, span_len, head_dim = span_keys.shape
    slot_count = retrieval.shape[1]
    recompute = tile_ids.shape[1]
    tile_len = tile_rows // recompute
    store_count = lax.axis_size("store")
    head_count = lax.axis_size("head")
    exp_scale = head_dim ** (-0.5) * math.log2(math.e)

    weights = lax.all_gather(
        jnp.concatenate([key_weight, value_weight], axis=1), "store", axis=0, tiled=True
    )

    store_rows = span_slot[retrieval]
    owners = store_rows // per_store
    hit = owners.reshape(1, -1) == jnp.arange(store_count, dtype=jnp.int32)[:, None]
    wanted = jnp.max(jnp.where(hit, (store_rows % per_store).reshape(1, -1), 0), axis=1)
    incoming = lax.all_to_all(
        wanted.reshape(store_count, 1), "store", split_axis=0, concat_axis=0, tiled=True
    )
    picked = pick_spans(incoming.reshape(-1), span_keys, span_values)
    got = lax.all_to_all(picked, "store", split_axis=0, concat_axis=0, tiled=True)

    queries = lax.all_to_all(
        split_columns(tile_queries, head_count), "head", split_axis=0, concat_axis=0, tiled=True
    )

    offsets = jnp.arange(tile_len, dtype=jnp.int32)
    positions = (tile_ids[:, :, None] * tile_len + offsets).reshape(-1)
    fresh_cos, fresh_sin = rope_tables(positions, head_dim)
    slot_cos, slot_sin = rope_tables(jnp.arange(slot_count, dtype=jnp.int32) * span_len, head_dim)

    acc, stat = stored_attention(owners, tile_ids, queries, got, slot_cos, slot_sin, exp_scale)
    fresh_keys, fresh_values = project(
        tile_inputs.reshape(queries_dev * tile_rows, width), weights, fresh_cos, fresh_sin
    )
    mixed = fresh_attention(tile_ids, queries, fresh_keys, fresh_values, acc, stat, exp_scale)
    return join_columns(
        lax.all_to_all(mixed, "head", split_axis=0, concat_axis=0, tiled=True)
    )


def solution(mesh):
    placed = (
        P("store", None, None),
        P("store", "head", None),
        P("store", "head"),
        P("store", "head"),
        P("store", "head", None, None),
        P("store", "head", None, None),
        P(),
        P("store", None),
        P("store", None),
    )
    return jax.shard_map(
        body, mesh=mesh, in_specs=placed, out_specs=P("store", "head", None), check_vma=False
    )
```

time: 400 us -> 352 us (0.88)
  Pallas kernels: 0 us -> 219 us
  matrix products: 99.9 us -> 0 us
  local copies, waits for them, and re-layouts: 93.3 us -> 3.24 us
  other arithmetic: 62.9 us -> 5.12 us
  blocking collectives: 81.8 us -> 31.3 us
  waiting for transfers between devices: 22.4 us -> 58.3 us
    pallas_call x0 -> x6, Pallas kernels: none -> 219 us  [the longest x1 129 us: pick_spans(): pl.pallas_call(pick_kernel, in_specs=[pl.BlockSpec(memory_space=pltpu.SME...]
    dot_general x6 -> x0, matrix products: 99.9 us -> none  [the longest x2 40.8 us: body(): jnp.einsum('rkgd,ksd->kgrs', grouped, key_block, preferred_element_type=j...]
    all_to_all x2 -> x1, blocking collectives: 81.8 us -> 31.3 us  [body(): lax.all_to_all(mixed, 'head', split_axis=0, concat_axis=0, tiled=True)]
    reduce_sum x4 -> x0, other arithmetic: 42.8 us -> none  [the longest x2 42.5 us: body(): row_total = jnp.sum(weights, axis=-1)]
    all_to_all x3, waiting for transfers between devices: 19.9 us -> 58.3 us  [the longest x1 58.3 us: body(): lax.all_to_all(picked, 'store', split_axis=0, concat_axis=0, tiled=True)]
    unnamed x15 -> x6, local copies, waits for them, and re-layouts: 30.8 us -> 1.73 us
    gather x6 -> x0, local copies, waits for them, and re-layouts: 21.4 us -> none  [the longest x2 7.74 us: body(): got_keys[owner_row, rank_row].astype(jnp.float32)]
    another operation x16 -> x0, local copies, waits for them, and re-layouts: 18.2 us -> none
  transfers between devices with their start and end apart: 5 -> 4, of which waited for: 3 -> 1; matrix products, arithmetic and copies ran while one was open for 26% -> 1% of each run, Pallas kernels for 0% -> 52%
where the time goes in v1:
time: 352 us; the launch traced here: 350 us
  Pallas kernels  219 us (62%)
  waiting for transfers between devices  58.3 us (17%)
  blocking collectives  31.3 us (9%)
  starting transfers between devices  20 us (6%)
  between operations  13.5 us (4%)
  other arithmetic  5.12 us (1%)
    pallas_call x1, Pallas kernels, pick_spans(): pl.pallas_call(pick_kernel, in_specs=[pl.BlockSpec(memory_space=pltpu.SME...  129 us
    all_to_all x1, waiting for transfers between devices, body(): lax.all_to_all(picked, 'store', split_axis=0, concat_axis=0, tiled=True)  58.3 us
    pallas_call x1, Pallas kernels, stored_attention(): pl.pallas_call(functools.partial(stored_kernel, exp_scale), grid_spec=plt...  48.8 us
    all_to_all x1, blocking collectives, body(): lax.all_to_all(mixed, 'head', split_axis=0, concat_axis=0, tiled=True)  31.3 us
    pallas_call x1, Pallas kernels, fresh_attention(): pl.pallas_call(functools.partial(fresh_kernel, exp_scale), grid_spec=pltp...  19.8 us
    pallas_call x1, Pallas kernels, project(): pl.pallas_call(project_kernel, grid=(width // depth,), in_specs=[pl.Block...  10.2 us
    all_to_all x1, starting transfers between devices, body(): lax.all_to_all(wanted.reshape(store_count, 1), 'store', split_axis=0, con...  8.27 us
    all_to_all x1, starting transfers between devices, body(): lax.all_to_all(picked, 'store', split_axis=0, concat_axis=0, tiled=True)  7.26 us
  transfers between devices with their start and end apart: 4, of which 1 were waited for; matrix products, arithmetic and copies ran while one was open for 1% of the time, Pallas kernels for 52%

profile of v1, /device:TPU:6, one launch (start us, length us, event | category | flops | bytes accessed | tf_op | source)
XLA Modules:
  0.0 350.1 jit_solution(6855587824185409779)
XLA Ops:
  6.5 0.0 copy-start
  6.5 0.0 all-gather.2.cloned.1.call-start
  6.5 1.8 pad_maximum_fusion
  8.4 0.0 all-gather.2.cloned.1.call-update
  8.4 0.7 compare_select_fusion
  9.1 0.1 reshape.94
  9.2 0.0 copy-done
  9.2 0.7 gather_fusion
  9.9 0.1 select_reduce_fusion
  10.0 0.7 copy.12
  10.7 8.3 %all-to-all-start.1 = ((s32[16,1,1]{2,1,0:T(1,128)}), s32[16,1,1]{2,1,0:T(1,128)S(1)}, u32[]{:S(2)}, u32[]{:S(2)}) async-start(s32[16,1,1]{2,1,0:T(1,128)} %copy.12), calls=%async_computation.1 | async-start | bytes 16384 | tf_op jit(solution)/shard_map/all_to_all | solution.py:324
  18.9 5.5 %split_columns.1 = bf16[8,2,32,1536]{3,2,1,0:T(8,128)(2,1)} custom-call(bf16[2,32,12288]{2,1,0:T(8,128)(2,1)} %x_ref.1), custom_call_target="tpu_custom_call" | custom-call | tf_op jit(solution)/shard_map/split_columns/pallas_call | solution.py:44
  24.4 0.0 all-to-all-done.1
  24.4 4.4 %all-to-all-start = ((bf16[8,2,32,1536]{3,2,1,0:T(8,128)(2,1)}), bf16[8,2,32,1536]{3,2,1,0:T(8,128)(2,1)S(1)}, u32[]{:S(2)}, u32[]{:S(2)}) async-start(bf16[8,2,32,1536]{3,2,1,0:T(8,128)(2,1)} %split_columns.1), calls=%async_computation | async-start | bytes 3145728 | tf_op jit(solution)/shard_map/all_to_all | solution.py:330
  28.8 1.0 reduce.rows_ref
  29.8 129.1 %pick_spans.1 = bf16[16,2,512,128]{3,2,1,0:T(8,128)(2,1)} custom-call(s32[16]{0:T(128)} %reduce.rows_ref, bf16[16,1,512,128]{3,2,1,0:T(8,128)(2,1)} %keys_ref.1, bf16[16,1,512,128]{3,2,1,0:T(8,128)(2,1)} %values_ref.1), custom_call_target="tpu_custom_call" | custom-call | tf_op jit(solution)/shard_map/pick_spans/pallas_call | solution.py:86
  158.9 0.0 copy-start.2
  158.9 0.0 all-to-all-done.q_ref
  159.0 7.3 %all-to-all-start.2 = ((bf16[16,2,512,128]{3,2,1,0:T(8,128)(2,1)}), bf16[16,2,512,128]{3,2,1,0:T(8,128)(2,1)}, u32[]{:S(2)}, u32[]{:S(2)}) async-start(bf16[16,2,512,128]{3,2,1,0:T(8,128)(2,1)} %pick_spans.1), calls=%async_computation.2 | async-start | bytes 8388608 | tf_op jit(solution)/shard_map/all_to_all | solution.py:328
  166.2 0.1 reshape.93
  166.3 0.1 fusion.1
  166.4 0.1 pad_maximum_fusion.3
  166.5 0.1 add_convert_fusion
  166.6 1.0 fusion
  167.6 0.2 pad_maximum_fusion.1
  167.8 58.3 %all-to-all-done.2.got_ref = bf16[16,2,512,128]{3,2,1,0:T(8,128)(2,1)} async-done(((bf16[16,2,512,128]{3,2,1,0:T(8,128)(2,1)}), bf16[16,2,512,128]{3,2,1,0:T(8,128)(2,1)}, u32[]{:S(2)}, u32[]{:S(2)}) %all-to-all-start.2) | async-done | bytes 4194336 | tf_op jit(solution)/shard_map/all_to_all | solution.py:328
  226.1 48.8 %stored_attention.1 = (f32[2,2,1536,128]{3,2,1,0:T(8,128)S(1)}, f32[2,2,1536,128]{3,2,1,0:T(8,128)}) custom-call(s32[2,8]{1,0:T(2,128)S(1)} %and_select_fusion.2.owner_ref, s32[2,2]{1,0:T(2,128)S(1)} %copy-done.2, bf16[8,2,32,1536]{3,2,1,0:T(8,128)(2,1)S(1)} %all-to-all-done.q_ref, bf16[16,2,512,128]{3,2,1,0:T(8,128)(2,1)} %all-to-all-done.2.got_ref, ...), custom_call_target="tpu_custom_call" | custom-call | flops 8000000000 | bytes 15000000 | tf_op jit(solution)/shard_map/stored_attention/pallas_call | solution.py:167
  274.9 1.7 copy-done.1
  276.6 10.2 %project.1 = (bf16[512,128]{1,0:T(8,128)(2,1)S(1)}, bf16[512,128]{1,0:T(8,128)(2,1)S(1)}) custom-call(bf16[512,12288]{1,0:T(8,128)(2,1)} %bitcast.3, bf16[12288,256]{1,0:T(8,128)(2,1)} %all-gather.2.cloned.1.call-done.w_ref, f32[512,128]{1,0:T(8,128)S(1)} %get-tuple-element.21.cos_ref, f32[512,128]{1,0:T(8,128)S(1)} %get-tuple-element.22.sin_ref), custom_call_target="tpu_custom_call" | custom-call | flops 3221225472 | bytes 18874368 | tf_op jit(solution)/shard_map/project/pallas_call | solution.py:216
  286.8 19.8 %fresh_attention.1 = bf16[8,2,32,1536]{3,2,1,0:T(8,128)(2,1)S(1)} custom-call(s32[2,2]{1,0:T(2,128)S(1)} %copy-done.2, bf16[8,2,32,1536]{3,2,1,0:T(8,128)(2,1)S(1)} %all-to-all-done.q_ref, bf16[512,128]{1,0:T(8,128)(2,1)S(1)} %get-tuple-element.9.keys_ref, bf16[512,128]{1,0:T(8,128)(2,1)S(1)} %get-tuple-element.10.values_ref, f32[2,2,1536,128]{3,2,1,0:T(8,128)} %copy-done.1, ...), custom_call_target="tpu_custom_call" | custom-call | flops 1000000000 | bytes 10000000 | tf_op jit(solution)/shard_map/fresh_attention/pallas_call | solution.py:279
  306.6 31.3 %all_to_all.24.x_ref = bf16[8,2,32,1536]{3,2,1,0:T(8,128)(2,1)} all-to-all(bf16[8,2,32,1536]{3,2,1,0:T(8,128)(2,1)S(1)} %fresh_attention.1), channel_id=1, replica_groups=mesh['store'=16,'head'=8] {'head'}, dimensions={0} | all-to-all | bytes 3145728 | tf_op jit(solution)/shard_map/all_to_all | solution.py:345
  337.9 5.4 %join_columns.1 = bf16[2,32,12288]{2,1,0:T(8,128)(2,1)} custom-call(bf16[8,2,32,1536]{3,2,1,0:T(8,128)(2,1)} %all_to_all.24.x_ref), custom_call_target="tpu_custom_call" | custom-call | tf_op jit(solution)/shard_map/join_columns/pallas_call | solution.py:60
  (9 shorter events, 0.1 us)
Async XLA Ops:
  6.5 2.6 copy-start
  6.5 270.1 %all-gather.2.cloned.1.call-start = ((), (), s32[]{:S(2)}) async-start(), calls=%async_computation.4 | async-start | bytes 6684672 | tf_op jit(solution)/shard_map/all_gather | solution.py:316
  10.7 13.7 %all-to-all-start.1 = ((s32[16,1,1]{2,1,0:T(1,128)}), s32[16,1,1]{2,1,0:T(1,128)S(1)}, u32[]{:S(2)}, u32[]{:S(2)}) async-start(s32[16,1,1]{2,1,0:T(1,128)} %copy.12), calls=%async_computation.1 | async-start | bytes 16384 | tf_op jit(solution)/shard_map/all_to_all | solution.py:324
  24.4 134.6 %all-to-all-start = ((bf16[8,2,32,1536]{3,2,1,0:T(8,128)(2,1)}), bf16[8,2,32,1536]{3,2,1,0:T(8,128)(2,1)S(1)}, u32[]{:S(2)}, u32[]{:S(2)}) async-start(bf16[8,2,32,1536]{3,2,1,0:T(8,128)(2,1)} %split_columns.1), calls=%async_computation | async-start | bytes 3145728 | tf_op jit(solution)/shard_map/all_to_all | solution.py:330
  158.9 7.6 %copy-start.2 = (s32[2,2]{1,0:T(2,128)S(1)}, s32[2,2]{1,0:T(2,128)}, u32[]{:S(2)}) copy-start(s32[2,2]{1,0:T(2,128)} %tile_ref.3) | copy-start | bytes 52
  159.0 67.1 %all-to-all-start.2 = ((bf16[16,2,512,128]{3,2,1,0:T(8,128)(2,1)}), bf16[16,2,512,128]{3,2,1,0:T(8,128)(2,1)}, u32[]{:S(2)}, u32[]{:S(2)}) async-start(bf16[16,2,512,128]{3,2,1,0:T(8,128)(2,1)} %pick_spans.1), calls=%async_computation.2 | async-start | bytes 8388608 | tf_op jit(solution)/shard_map/all_to_all | solution.py:328
  274.9 1.7 copy-start.1
Sparse Core Ops, SparseCore 0:
  9.5 63.7 all-gather.1

commit v2 on v1

v2 whole, which is shorter than its diff:
```python
import functools
import math

import jax
import jax.numpy as jnp
from jax import lax
from jax.experimental import pallas as pl
from jax.experimental.pallas import tpu as pltpu
from jax.sharding import PartitionSpec as P

rope_base = 1000000.0
low = -1e30


def rope_tables(positions, width):
    half_width = width // 2
    exponent = jnp.arange(half_width, dtype=jnp.float32) * (2.0 / width)
    frequency = jnp.power(jnp.float32(rope_base), -exponent)
    angle = positions.astype(jnp.float32)[..., None] * frequency
    cosine = jnp.cos(angle)
    sine = jnp.sin(angle)
    return (
        jnp.concatenate([cosine, cosine], axis=-1),
        jnp.concatenate([-sine, sine], axis=-1),
    )


def rotate(values, cosine, signed_sine):
    swapped = pltpu.roll(values, values.shape[-1] // 2, 1)
    return values * cosine + swapped * signed_sine


def whole(shape):
    return pl.BlockSpec(shape, lambda *_: (0,) * len(shape))


def head_partner(me, step, count, sign):
    ring = count // 2
    turn = lax.rem(me // 2 + sign * (step // 2) + ring, ring)
    return 2 * turn + lax.rem(lax.rem(me, 2) + lax.rem(step, 2), 2)


def split_kernel(x_ref, *o_refs):
    me = lax.axis_index("head")
    part = o_refs[0].shape[2]
    for step, o_ref in enumerate(o_refs):
        to = head_partner(me, step, len(o_refs), 1)
        o_ref[...] = x_ref[:, :, pl.ds(pl.multiple_of(to * part, part), part)]


def split_columns(x, pieces):
    lead, rows, width = x.shape
    out = jax.ShapeDtypeStruct((lead, rows, width // pieces), x.dtype)
    return pl.pallas_call(split_kernel, out_shape=[out] * pieces, name="split_columns")(x)


def assemble_kernel(*refs):
    pieces = refs[:-2]
    o_ref, staged = refs[-2:]
    me = lax.axis_index("head")
    for step, piece in enumerate(pieces):
        staged[head_partner(me, step, len(pieces), -1)] = piece[...]
    queries_dev, recompute, double, all_rows = o_ref.shape
    head_dim = double // 2
    sources, _, rows, part = staged.shape
    per_tile = sources // recompute
    tile_len = per_tile * rows
    marker = (lax.broadcasted_iota(jnp.int32, (head_dim, all_rows), 0) == 0).astype(jnp.bfloat16)
    for i in range(queries_dev):
        for j in range(recompute):
            tile = staged[j * per_tile : (j + 1) * per_tile, i].reshape(tile_len, part)
            for g in range(part // head_dim):
                o_ref[i, j, :head_dim, g * tile_len : (g + 1) * tile_len] = tile[
                    :, g * head_dim : (g + 1) * head_dim
                ].T
            o_ref[i, j, head_dim:, :] = marker


def assemble(pieces, recompute, head_dim):
    queries_dev, rows, part = pieces[0].shape
    all_rows = len(pieces) // recompute * rows * (part // head_dim)
    return pl.pallas_call(
        assemble_kernel,
        out_shape=jax.ShapeDtypeStruct((queries_dev, recompute, 2 * head_dim, all_rows), pieces[0].dtype),
        scratch_shapes=[pltpu.VMEM((len(pieces),) + pieces[0].shape, pieces[0].dtype)],
        compiler_params=pltpu.CompilerParams(vmem_limit_bytes=20 * 2**20),
        name="assemble",
    )(*pieces)


def join_kernel(x_ref, o_ref):
    part = x_ref.shape[3]
    for j in range(x_ref.shape[0]):
        o_ref[:, :, j * part : (j + 1) * part] = x_ref[j]


def join_columns(x):
    pieces, lead, rows, part = x.shape
    return pl.pallas_call(
        join_kernel,
        out_shape=jax.ShapeDtypeStruct((lead, rows, pieces * part), x.dtype),
        name="join_columns",
    )(x)


def pick_kernel(rows_ref, keys_ref, values_ref, *o_refs):
    def step(d, carry):
        row = rows_ref[d]
        start = 0
        for o_ref in o_refs:
            at = slice(start, start + o_ref.shape[2])
            o_ref[d, 0] = keys_ref[row, 0, at]
            o_ref[d, 1] = values_ref[row, 0, at]
            start = at.stop
        return carry

    lax.fori_loop(0, o_refs[0].shape[0], step, 0)


def pick_spans(rows, keys, values, pieces):
    count = rows.shape[0]
    span_len, head_dim = keys.shape[2:]
    out = jax.ShapeDtypeStruct((count, 2, span_len // pieces, head_dim), keys.dtype)
    return pl.pallas_call(
        pick_kernel,
        in_specs=[
            pl.BlockSpec(memory_space=pltpu.SMEM),
            pl.BlockSpec(memory_space=pltpu.VMEM),
            pl.BlockSpec(memory_space=pltpu.VMEM),
        ],
        out_specs=[pl.BlockSpec(memory_space=pltpu.VMEM)] * pieces,
        out_shape=[out] * pieces,
        compiler_params=pltpu.CompilerParams(vmem_limit_bytes=20 * 2**20),
        name="pick_spans",
    )(rows, keys, values)


def blend(scores, before, exp_scale):
    after = jnp.maximum(before, jnp.max(scores, axis=0, keepdims=True))
    weights = jnp.exp2((scores - after) * exp_scale).astype(jnp.bfloat16)
    fade = jnp.exp2((before - after) * exp_scale)
    return after, weights, fade


def add_keys(exp_scale, q_ref, acc_ref, top_ref, keys, values, bias, wide):
    all_rows = q_ref.shape[3]
    depth = keys.shape[1]
    ones = jnp.ones((acc_ref.shape[2] - values.shape[1], keys.shape[0]), jnp.bfloat16)
    values = jnp.concatenate([values.T, ones], axis=0)
    blocks = [pl.ds(start, wide) for start in range(0, all_rows, wide)]
    scores = {}
    for turn in range(-1, len(blocks)):
        if turn + 1 < len(blocks):
            scores[turn + 1] = jnp.dot(
                keys, q_ref[0, 0, :depth, blocks[turn + 1]], preferred_element_type=jnp.float32
            )
        if turn >= 0:
            at = blocks[turn]
            now = scores.pop(turn)
            if bias is not None:
                now = now + bias
            after, weights, fade = blend(now, top_ref[0, 0, :1, at], exp_scale)
            top_ref[0, 0, :1, at] = after
            acc_ref[0, 0, :, at] = acc_ref[0, 0, :, at] * fade + jnp.dot(
                values, weights, preferred_element_type=jnp.float32
            )


def attend_kernel(exp_scale, tile_len, piece, pieces, fresh, started, finish, *refs):
    refs = list(refs)
    owner_ref, tile_ref, q_ref = refs[:3]
    del refs[:3]
    query = pl.program_id(0)
    number = pl.program_id(1)
    own = tile_ref[query, number]
    other = tile_ref[query, 1 - number]
    if piece is not None:
        got_ref, cos_ref, sin_ref = refs[:3]
        del refs[:3]
    if fresh:
        keys_ref, values_ref = refs[:2]
        del refs[:2]
    if started:
        acc_in, top_in = refs[:2]
        del refs[:2]
    if finish:
        o_ref = refs.pop(0)
    acc_ref, top_ref = refs
    head_dim = q_ref.shape[2] // 2
    wide = 4 * tile_len
    all_rows = q_ref.shape[3]
    if started:
        acc_ref[...] = acc_in[...]
        top_ref[...] = top_in[...]
    else:
        top_ref[...] = jnp.full_like(top_ref, low)
        acc_ref[...] = jnp.zeros_like(acc_ref)
    if piece is not None:
        part_len = got_ref.shape[2]
        per_part = part_len // tile_len
        per_span = per_part * pieces
        key_lane = lax.broadcasted_iota(jnp.int32, (part_len, head_dim), 1)
        key_row = lax.broadcasted_iota(jnp.int32, (part_len, head_dim), 0)

        def step(group, carry):
            key_parts = []
            value_parts = []
            for inner in range(pieces):
                p = group * pieces + inner
                owner = owner_ref[query, p]
                turned = rotate(
                    got_ref[owner, 0].astype(jnp.float32),
                    cos_ref[pl.ds(p, 1), :],
                    sin_ref[pl.ds(p, 1), :],
                ).astype(jnp.bfloat16)
                key_tile = p * per_span + piece * per_part + key_row // tile_len
                hidden = (key_lane == 0) & ((key_tile >= own) | (key_tile == other))
                key_parts.append(
                    jnp.concatenate(
                        [turned, jnp.where(hidden, low, 0.0).astype(jnp.bfloat16)], axis=1
                    )
                )
                value_parts.append(got_ref[owner, 1])
            keys = jnp.concatenate(key_parts, axis=0)
            values = jnp.concatenate(value_parts, axis=0)
            add_keys(exp_scale, q_ref, acc_ref, top_ref, keys, values, None, wide)
            return carry

        spans = (own - piece * per_part + per_span - 1) // per_span
        lax.fori_loop(0, (spans + pieces - 1) // pieces, step, 0)
    if fresh:
        rows = keys_ref.shape[0]
        key = lax.broadcasted_iota(jnp.int32, (rows, tile_len), 0)
        row = lax.broadcasted_iota(jnp.int32, (rows, tile_len), 1)
        in_own = key // tile_len == number
        allowed = (in_own & (key % tile_len <= row)) | (jnp.logical_not(in_own) & (other < own))
        bias = jnp.concatenate([jnp.where(allowed, 0.0, low)] * (wide // tile_len), axis=1)
        add_keys(exp_scale, q_ref, acc_ref, top_ref, keys_ref[...], values_ref[...], bias, wide)
    if finish:
        for start in range(0, all_rows, wide):
            at = pl.ds(start, wide)
            result = acc_ref[0, 0, :head_dim, at] / acc_ref[0, 0, head_dim : head_dim + 1, at]
            result = result.astype(jnp.bfloat16).T
            for h in range(0, wide, tile_len):
                column = (start + h) // tile_len * head_dim
                o_ref[:, 0, :, column : column + head_dim] = result[h : h + tile_len].reshape(
                    o_ref.shape[0], o_ref.shape[2], head_dim
                )


def attend(owner, tile_ids, queries, exp_scale, tile_len, sources=None, stored=None, piece=None, pieces=1, fresh=None, state=None):
    queries_dev, recompute, double, all_rows = queries.shape
    head_dim = double // 2
    args = [queries]
    specs = [pl.BlockSpec((1, 1, double, all_rows), lambda i, j, *_: (i, j, 0, 0))]
    if stored is not None:
        args += stored
        specs += [whole(x.shape) for x in stored]
    if fresh is not None:
        args += fresh
        specs += [
            pl.BlockSpec((x.shape[0] // queries_dev, head_dim), lambda i, j, *_: (i, 0)) for x in fresh
        ]
    shapes = [(head_dim + 16, all_rows), (8, all_rows)]
    state_specs = [pl.BlockSpec((1, 1) + shape, lambda i, j, *_: (i, j, 0, 0)) for shape in shapes]
    if state is not None:
        args += state
        specs += state_specs
    if sources is None:
        out_shape = [
            jax.ShapeDtypeStruct((queries_dev, recompute) + shape, jnp.float32) for shape in shapes
        ]
        out_specs = state_specs
        scratch = []
    else:
        rows = recompute * tile_len // sources
        part = all_rows // tile_len * head_dim
        out_shape = jax.ShapeDtypeStruct((sources, queries_dev, rows, part), queries.dtype)
        out_specs = pl.BlockSpec((sources // recompute, 1, rows, part), lambda i, j, *_: (j, i, 0, 0))
        scratch = [pltpu.VMEM((1, 1) + shape, jnp.float32) for shape in shapes]
    return pl.pallas_call(
        functools.partial(
            attend_kernel, exp_scale, tile_len, piece, pieces, fresh is not None, state is not None, sources is not None
        ),
        grid_spec=pltpu.PrefetchScalarGridSpec(
            num_scalar_prefetch=2,
            grid=(queries_dev, recompute),
            in_specs=specs,
            out_specs=out_specs,
            scratch_shapes=scratch,
        ),
        out_shape=out_shape,
        compiler_params=pltpu.CompilerParams(vmem_limit_bytes=24 * 2**20),
        cost_estimate=pl.CostEstimate(
            flops=16 * 10**9 // pieces if stored is not None else 10**9,
            bytes_accessed=15 * 10**6 // pieces,
            transcendentals=16 * 10**6 // pieces,
        ),
        name="attend" + ("_stored" if stored is not None else "") + ("_fresh" if fresh is not None else ""),
    )(owner, tile_ids, *args)


def project_kernel(x_ref, w_ref, cos_ref, sin_ref, keys_ref, values_ref, total):
    step = pl.program_id(0)
    head_dim = keys_ref.shape[1]

    @pl.when(step == 0)
    def _():
        total[...] = jnp.zeros_like(total)

    total[...] += jnp.dot(x_ref[...], w_ref[...], preferred_element_type=jnp.float32)

    @pl.when(step == pl.num_programs(0) - 1)
    def _():
        keys_ref[...] = rotate(total[:, :head_dim], cos_ref[...], sin_ref[...]).astype(jnp.bfloat16)
        values_ref[...] = total[:, head_dim:].astype(jnp.bfloat16)


def project(x, weights, cosine, signed_sine):
    rows, width = x.shape
    columns = weights.shape[1]
    head_dim = columns // 2
    depth = 3072
    out = jax.ShapeDtypeStruct((rows, head_dim), jnp.bfloat16)
    return pl.pallas_call(
        project_kernel,
        grid=(width // depth,),
        in_specs=[
            pl.BlockSpec((rows, depth), lambda k: (0, k)),
            pl.BlockSpec((depth, columns), lambda k: (k, 0)),
            whole(cosine.shape),
            whole(signed_sine.shape),
        ],
        out_specs=[whole(out.shape), whole(out.shape)],
        out_shape=[out, out],
        scratch_shapes=[pltpu.VMEM((rows, columns), jnp.float32)],
        compiler_params=pltpu.CompilerParams(vmem_limit_bytes=20 * 2**20),
        cost_estimate=pl.CostEstimate(
            flops=2 * rows * width * columns, bytes_accessed=2 * width * (rows + columns), transcendentals=0
        ),
        name="project",
    )(x, weights, cosine, signed_sine)


def body(
    tile_inputs,
    tile_queries,
    key_weight,
    value_weight,
    span_keys,
    span_values,
    span_slot,
    retrieval,
    tile_ids,
):
    queries_dev, tile_rows, width = tile_inputs.shape
    per_store, _, span_len, head_dim = span_keys.shape
    slot_count = retrieval.shape[1]
    recompute = tile_ids.shape[1]
    tile_len = tile_rows // recompute
    store_count = lax.axis_size("store")
    head_count = lax.axis_size("head")
    exp_scale = head_dim ** (-0.5) * math.log2(math.e)

    store_rows = span_slot[retrieval]
    owners = store_rows // per_store
    hit = owners.reshape(1, -1) == jnp.arange(store_count, dtype=jnp.int32)[:, None]
    wanted = jnp.max(jnp.where(hit, (store_rows % per_store).reshape(1, -1), 0), axis=1)
    incoming = lax.all_to_all(
        wanted.reshape(store_count, 1), "store", split_axis=0, concat_axis=0, tiled=True
    )
    weights = lax.all_gather(
        jnp.concatenate([key_weight, value_weight], axis=1), "store", axis=0, tiled=True
    )
    pieces = 2
    picked = pick_spans(incoming.reshape(-1), span_keys, span_values, pieces)
    split = split_columns(tile_queries, head_count)
    ring = head_count // 2
    received = [split[0]]
    for step in range(1, head_count):
        pairs = [
            (me, 2 * ((me // 2 + step // 2) % ring) + (me + step) % 2) for me in range(head_count)
        ]
        received.append(lax.ppermute(split[step], "head", pairs))
    queries = assemble(received, recompute, head_dim)

    got = []
    for part in picked:
        if got:
            part, queries = lax.optimization_barrier((part, queries))
        got.append(lax.all_to_all(part, "store", split_axis=0, concat_axis=0, tiled=True))

    offsets = jnp.arange(tile_len, dtype=jnp.int32)
    positions = (tile_ids[:, :, None] * tile_len + offsets).reshape(-1)
    fresh_cos, fresh_sin = rope_tables(positions, head_dim)
    slot_cos, slot_sin = rope_tables(jnp.arange(slot_count, dtype=jnp.int32) * span_len, head_dim)

    fresh = project(
        tile_inputs.reshape(queries_dev * tile_rows, width), weights, fresh_cos, fresh_sin
    )
    run = functools.partial(attend, owners, tile_ids, queries, exp_scale, tile_len)
    turn = [slot_cos, slot_sin]
    state = run(stored=[got[0]] + turn, piece=0, pieces=pieces)
    state = run(fresh=fresh, state=state)
    mixed = run(stored=[got[1]] + turn, piece=1, pieces=pieces, state=state, sources=head_count)
    return join_columns(
        lax.all_to_all(mixed, "head", split_axis=0, concat_axis=0, tiled=True)
    )


def solution(mesh):
    placed = (
        P("store", None, None),
        P("store", "head", None),
        P("store", "head"),
        P("store", "head"),
        P("store", "head", None, None),
        P("store", "head", None, None),
        P(),
        P("store", None),
        P("store", None),
    )
    return jax.shard_map(
        body, mesh=mesh, in_specs=placed, out_specs=P("store", "head", None), check_vma=False
    )
```

time: 352 us -> 186 us (0.53)
  the two profiles are of different devices: /device:TPU:6 before, /device:TPU:4 now
where the time goes in v2:
time: 186 us; the launch traced here: 188 us
  Pallas kernels  60.2 us (32%)
  blocking collectives  39.8 us (21%)
  starting transfers between devices  24.8 us (13%)
  waiting for transfers between devices  23.6 us (13%)
  local copies, waits for them, and re-layouts  20.6 us (11%)
  between operations  13.5 us (7%)
  other arithmetic  5.33 us (3%)
    pallas_call x3, Pallas kernels, attend(): pl.pallas_call(functools.partial(attend_kernel, exp_scale, tile_len, piec...  48.3 us
    all_to_all x1, blocking collectives, body(): lax.all_to_all(mixed, 'head', split_axis=0, concat_axis=0, tiled=True)  26.4 us
    unnamed x32, local copies, waits for them, and re-layouts  19.7 us
    all_to_all x2, starting transfers between devices, body(): lax.all_to_all(part, 'store', split_axis=0, concat_axis=0, tiled=True)  16.1 us
    ppermute x7, waiting for transfers between devices, body(): received.append(lax.ppermute(split[step], 'head', pairs))  13.9 us
    all_to_all x1, blocking collectives, body(): lax.all_to_all(wanted.reshape(store_count, 1), 'store', split_axis=0, con...  13.4 us
    all_to_all x2, waiting for transfers between devices, body(): lax.all_to_all(part, 'store', split_axis=0, concat_axis=0, tiled=True)  9.61 us
    ppermute x7, starting transfers between devices, body(): received.append(lax.ppermute(split[step], 'head', pairs))  8.73 us
  transfers between devices with their start and end apart: 10, of which 6 were waited for; matrix products, arithmetic and copies ran while one was open for 2% of the time, Pallas kernels for 19%

profile of v2, /device:TPU:4, one launch (start us, length us, event | category | flops | bytes accessed | tf_op | source)
XLA Modules:
  0.0 187.9 jit_solution(10942989673706596297)
XLA Ops:
  6.5 2.0 %pad_maximum_fusion = bf16[768,256]{1,0:T(8,128)(2,1)} fusion(bf16[768,128]{1,0:T(8,128)(2,1)} %param.12, bf16[768,128]{1,0:T(8,128)(2,1)} %param.11), kind=kLoop, calls=%fused_computation.1 | loop fusion | flops 786432 | bytes 786432 | tf_op jit(solution)/shard_map/concatenate | solution.py:373
  10.2 13.4 %all_to_all.24 = s32[16,1,1]{2,1,0:T(1,128)S(1)} all-to-all(s32[16,1,1]{2,1,0:T(1,128)S(1)} %copy.12), channel_id=1, replica_groups=mesh['store'=16,'head'=8] {'store'}, dimensions={0} | all-to-all | bytes 128 | tf_op jit(solution)/shard_map/all_to_all | solution.py:369
  24.0 1.6 copy-done.4
  26.5 1.3 copy-done.5
  27.7 1.4 copy-done.6
  29.1 6.7 %all-to-all-start.2 = ((bf16[16,2,256,128]{3,2,1,0:T(8,128)(2,1)}), bf16[16,2,256,128]{3,2,1,0:T(8,128)(2,1)}, u32[]{:S(2)}, u32[]{:S(2)}) async-start(bf16[16,2,256,128]{3,2,1,0:T(8,128)(2,1)} %copy-done.6), calls=%async_computation.2 | async-start | bytes 4194304 | tf_op jit(solution)/shard_map/all_to_all | solution.py:391
  35.8 2.7 %split_columns.1 = (bf16[2,32,1536]{2,1,0:T(8,128)(2,1)}, bf16[2,32,1536]{2,1,0:T(8,128)(2,1)}, bf16[2,32,1536]{2,1,0:T(8,128)(2,1)}, bf16[2,32,1536]{2,1,0:T(8,...) custom-call(bf16[2,32,12288]{2,1,0:T(8,128)(2,1)} %x_ref.1), custom_call_target="tpu_custom_call" | custom-call | tf_op jit(solution)/shard_map/split_columns/pallas_call | solution.py:54
  38.5 1.6 collective-permute-start.1
  40.1 1.4 collective-permute-start.2
  41.5 1.6 collective-permute-start.3
  43.1 1.5 collective-permute-start.4
  44.8 1.7 collective-permute-start.5
  46.5 1.1 collective-permute-done.1.refs_2_
  48.5 2.7 %collective-permute-done.2.refs_3_ = bf16[2,32,1536]{2,1,0:T(8,128)(2,1)S(1)} collective-permute-done((bf16[2,32,1536]{2,1,0:T(8,128)(2,1)}, bf16[2,32,1536]{2,1,0:T(8,128)(2,1)S(1)}, u32[]{:S(2)}, u32[]{:S(2)}) %collective-permute-start.2) | collective-permute-done | bytes 196640 | tf_op jit(solution)/shard_map/ppermute | solution.py:384
  51.2 6.1 %collective-permute-done.3.refs_4_ = bf16[2,32,1536]{2,1,0:T(8,128)(2,1)S(1)} collective-permute-done((bf16[2,32,1536]{2,1,0:T(8,128)(2,1)}, bf16[2,32,1536]{2,1,0:T(8,128)(2,1)S(1)}, u32[]{:S(2)}, u32[]{:S(2)}) %collective-permute-start.3) | collective-permute-done | bytes 196640 | tf_op jit(solution)/shard_map/ppermute | solution.py:384
  57.3 3.4 %collective-permute-done.4.refs_5_ = bf16[2,32,1536]{2,1,0:T(8,128)(2,1)S(1)} collective-permute-done((bf16[2,32,1536]{2,1,0:T(8,128)(2,1)}, bf16[2,32,1536]{2,1,0:T(8,128)(2,1)S(1)}, u32[]{:S(2)}, u32[]{:S(2)}) %collective-permute-start.4) | collective-permute-done | bytes 196640 | tf_op jit(solution)/shard_map/ppermute | solution.py:384
  61.3 0.9 copy-done.8
  62.9 9.6 %all-to-all-done.2.refs_3_ = bf16[16,2,256,128]{3,2,1,0:T(8,128)(2,1)} async-done(((bf16[16,2,256,128]{3,2,1,0:T(8,128)(2,1)}), bf16[16,2,256,128]{3,2,1,0:T(8,128)(2,1)}, u32[]{:S(2)}, u32[]{:S(2)}) %all-to-all-start.2) | async-done | bytes 2097184 | tf_op jit(solution)/shard_map/all_to_all | solution.py:391
  72.5 9.4 %all-to-all-start.1 = ((bf16[16,2,256,128]{3,2,1,0:T(8,128)(2,1)}), bf16[16,2,256,128]{3,2,1,0:T(8,128)(2,1)}, u32[]{:S(2)}, u32[]{:S(2)}) async-start(bf16[16,2,256,128]{3,2,1,0:T(8,128)(2,1)} %copy-done.5), calls=%async_computation.1 | async-start | bytes 4194304 | tf_op jit(solution)/shard_map/all_to_all | solution.py:391
  82.1 1.0 fusion
  84.0 21.2 %attend_stored.2 = (f32[2,2,144,1536]{3,2,1,0:T(8,128)S(1)}, f32[2,2,8,1536]{3,2,1,0:T(8,128)S(1)}) custom-call(s32[2,8]{1,0:T(2,128)S(1)} %and_select_fusion.2.refs_0_, s32[2,2]{1,0:T(2,128)S(1)} %copy-done.9, bf16[2,2,256,1536]{3,2,1,0:T(8,128)(2,1)S(1)} %assemble.1.refs_2_, bf16[16,2,256,128]{3,2,1,0:T(8,128)(2,1)} %all-to-all-done.2.refs_3_, ...), custom_call_target="tpu_custom_call" | custom-call | flops 8000000000 | bytes 7500000 | tf_op jit(solution)/shard_map/attend_stored/pallas_call | solution.py:281
  105.3 1.8 copy-done.12
  107.8 4.6 %copy-done.1 = bf16[2,256,12288]{2,1,0:T(8,128)(2,1)S(1)} copy-done((bf16[2,256,12288]{2,1,0:T(8,128)(2,1)S(1)}, bf16[2,256,12288]{2,1,0:T(8,128)(2,1)}, u32[]{:S(2)}) %copy-start.1) | copy-done | bytes 12582936
  112.4 2.8 %copy-done.2 = bf16[12288,256]{1,0:T(8,128)(2,1)S(1)} copy-done((bf16[12288,256]{1,0:T(8,128)(2,1)S(1)}, bf16[12288,256]{1,0:T(8,128)(2,1)}, u32[]{:S(2)}) %copy-start.2) | copy-done | bytes 6291480
  115.1 0.9 copy-done.7
  116.1 5.0 %project.1 = (bf16[512,128]{1,0:T(8,128)(2,1)S(1)}, bf16[512,128]{1,0:T(8,128)(2,1)S(1)}) custom-call(bf16[512,12288]{1,0:T(8,128)(2,1)S(1)} %bitcast.3, bf16[12288,256]{1,0:T(8,128)(2,1)S(1)} %copy-done.2, f32[512,128]{1,0:T(8,128)S(1)} %get-tuple-element.51.cos_ref, f32[512,128]{1,0:T(8,128)S(1)} %copy-done.7), custom_call_target="tpu_custom_call" | custom-call | flops 3221225472 | bytes 18874368 | tf_op jit(solution)/shard_map/project/pallas_call | solution.py:325
  121.1 5.2 %attend_fresh.1 = (f32[2,2,144,1536]{3,2,1,0:T(8,128)S(1)}, f32[2,2,8,1536]{3,2,1,0:T(8,128)S(1)}) custom-call(s32[2,8]{1,0:T(2,128)S(1)} %and_select_fusion.2.refs_0_, s32[2,2]{1,0:T(2,128)S(1)} %copy-done.9, bf16[2,2,256,1536]{3,2,1,0:T(8,128)(2,1)S(1)} %assemble.1.refs_2_, bf16[512,128]{1,0:T(8,128)(2,1)S(1)} %get-tuple-element.34.refs_3_, ...), custom_call_target="tpu_custom_call" | custom-call | flops 1000000000 | bytes 15000000 | tf_op jit(solution)/shard_map/attend_fresh/pallas_call | solution.py:281
  126.3 1.7 copy-done.10
  128.1 2.0 %copy-done.11 = f32[2,2,144,1536]{3,2,1,0:T(8,128)S(1)} copy-done((f32[2,2,144,1536]{3,2,1,0:T(8,128)S(1)}, f32[2,2,144,1536]{3,2,1,0:T(8,128)}, u32[]{:S(2)}) %copy-start.11) | copy-done | bytes 3538968
  130.1 21.9 %attend_stored.3 = bf16[8,2,32,1536]{3,2,1,0:T(8,128)(2,1)S(1)} custom-call(s32[2,8]{1,0:T(2,128)S(1)} %and_select_fusion.2.refs_0_, s32[2,2]{1,0:T(2,128)S(1)} %copy-done.9, bf16[2,2,256,1536]{3,2,1,0:T(8,128)(2,1)S(1)} %assemble.1.refs_2_, bf16[16,2,256,128]{3,2,1,0:T(8,128)(2,1)} %all-to-all-done.1.refs_3_, f32[8,128]{1,0:T(8,128)S(1)} %get-tuple-element.49.refs_4_, ...), custom_call_target="tpu_custom_call" | custom-call | flops 8000000000 | bytes 7500000 | tf_op jit(solution)/shard_map/attend_stored/pallas_call | solution.py:281
  152.0 26.4 %all_to_all.25.x_ref = bf16[8,2,32,1536]{3,2,1,0:T(8,128)(2,1)} all-to-all(bf16[8,2,32,1536]{3,2,1,0:T(8,128)(2,1)S(1)} %attend_stored.3), channel_id=1, replica_groups=mesh['store'=16,'head'=8] {'head'}, dimensions={0} | all-to-all | bytes 3145728 | tf_op jit(solution)/shard_map/all_to_all | solution.py:407
  178.4 2.7 %join_columns.1 = bf16[2,32,12288]{2,1,0:T(8,128)(2,1)} custom-call(bf16[8,2,32,1536]{3,2,1,0:T(8,128)(2,1)} %all_to_all.25.x_ref), custom_call_target="tpu_custom_call" | custom-call | tf_op jit(solution)/shard_map/join_columns/pallas_call | solution.py:99
  (50 shorter events, 7.0 us)
Async XLA Ops:
  6.5 2.8 %copy-start = (s32[256]{0:T(256)S(1)}, s32[256]{0:T(256)}, u32[]{:S(2)}) copy-start(s32[256]{0:T(256)} %param.15) | copy-start | bytes 3076
  6.5 17.4 %copy-start.3 = (bf16[16,1,512,128]{3,2,1,0:T(8,128)(2,1)S(1)}, bf16[16,1,512,128]{3,2,1,0:T(8,128)(2,1)}, u32[]{:S(2)}) copy-start(bf16[16,1,512,128]{3,2,1,0:T(8,128)(2,1)} %keys_ref.1) | copy-start | bytes 6291460
  6.5 101.2 %all-gather.2.cloned.1.call-start = ((), (), s32[]{:S(2)}) async-start(), calls=%async_computation.4 | async-start | bytes 6684672 | tf_op jit(solution)/shard_map/all_gather | solution.py:372
  24.0 1.6 copy-start.4
  26.5 1.3 copy-start.5
  27.7 1.4 copy-start.6
  29.1 19.4 %copy-start.9 = (s32[2,2]{1,0:T(2,128)S(1)}, s32[2,2]{1,0:T(2,128)}, u32[]{:S(2)}) copy-start(s32[2,2]{1,0:T(2,128)} %refs_1_.5) | copy-start | bytes 52
  29.1 43.4 %all-to-all-start.2 = ((bf16[16,2,256,128]{3,2,1,0:T(8,128)(2,1)}), bf16[16,2,256,128]{3,2,1,0:T(8,128)(2,1)}, u32[]{:S(2)}, u32[]{:S(2)}) async-start(bf16[16,2,256,128]{3,2,1,0:T(8,128)(2,1)} %copy-done.6), calls=%async_computation.2 | async-start | bytes 4194304 | tf_op jit(solution)/shard_map/all_to_all | solution.py:391
  38.5 6.3 %collective-permute-start = (bf16[2,32,1536]{2,1,0:T(8,128)(2,1)}, bf16[2,32,1536]{2,1,0:T(8,128)(2,1)S(1)}, u32[]{:S(2)}, u32[]{:S(2)}) collective-permute-start(bf16[2,32,1536]{2,1,0:T(8,128)(2,1)} %get-tuple-element.25), channel_id=1, source_target_pairs={{0,1},{1,0},{2,3},{3,2},{4,5},{5,4},{6,7},{7,6},{8,9},{9,8},{10,11... | collective-permute-start | bytes 589832 | tf_op jit(solution)/shard_map/ppermute | solution.py:384
  38.5 9.1 %collective-permute-start.1 = (bf16[2,32,1536]{2,1,0:T(8,128)(2,1)}, bf16[2,32,1536]{2,1,0:T(8,128)(2,1)S(1)}, u32[]{:S(2)}, u32[]{:S(2)}) collective-permute-start(bf16[2,32,1536]{2,1,0:T(8,128)(2,1)} %get-tuple-element.26), channel_id=1, source_target_pairs={{0,2},{1,3},{2,4},{3,5},{4,6},{5,7},{6,0},{7,1},{8,10},{9,11},{10,... | collective-permute-start | bytes 589832 | tf_op jit(solution)/shard_map/ppermute | solution.py:384
  40.1 11.1 %collective-permute-start.2 = (bf16[2,32,1536]{2,1,0:T(8,128)(2,1)}, bf16[2,32,1536]{2,1,0:T(8,128)(2,1)S(1)}, u32[]{:S(2)}, u32[]{:S(2)}) collective-permute-start(bf16[2,32,1536]{2,1,0:T(8,128)(2,1)} %get-tuple-element.27), channel_id=1, source_target_pairs={{0,3},{1,2},{2,5},{3,4},{4,7},{5,6},{6,1},{7,0},{8,11},{9,10},{10,... | collective-permute-start | bytes 589832 | tf_op jit(solution)/shard_map/ppermute | solution.py:384
  41.5 15.8 %collective-permute-start.3 = (bf16[2,32,1536]{2,1,0:T(8,128)(2,1)}, bf16[2,32,1536]{2,1,0:T(8,128)(2,1)S(1)}, u32[]{:S(2)}, u32[]{:S(2)}) collective-permute-start(bf16[2,32,1536]{2,1,0:T(8,128)(2,1)} %get-tuple-element.28), channel_id=1, source_target_pairs={{0,4},{1,5},{2,6},{3,7},{4,0},{5,1},{6,2},{7,3},{8,12},{9,13},{10,... | collective-permute-start | bytes 589832 | tf_op jit(solution)/shard_map/ppermute | solution.py:384
  43.1 17.6 %collective-permute-start.4 = (bf16[2,32,1536]{2,1,0:T(8,128)(2,1)}, bf16[2,32,1536]{2,1,0:T(8,128)(2,1)S(1)}, u32[]{:S(2)}, u32[]{:S(2)}) collective-permute-start(bf16[2,32,1536]{2,1,0:T(8,128)(2,1)} %get-tuple-element.29), channel_id=1, source_target_pairs={{0,5},{1,4},{2,7},{3,6},{4,1},{5,0},{6,3},{7,2},{8,13},{9,12},{10,... | collective-permute-start | bytes 589832 | tf_op jit(solution)/shard_map/ppermute | solution.py:384
  44.8 16.0 %collective-permute-start.5 = (bf16[2,32,1536]{2,1,0:T(8,128)(2,1)}, bf16[2,32,1536]{2,1,0:T(8,128)(2,1)S(1)}, u32[]{:S(2)}, u32[]{:S(2)}) collective-permute-start(bf16[2,32,1536]{2,1,0:T(8,128)(2,1)} %get-tuple-element.30), channel_id=1, source_target_pairs={{0,6},{1,7},{2,0},{3,1},{4,2},{5,3},{6,4},{7,5},{8,14},{9,15},{10,... | collective-permute-start | bytes 589832 | tf_op jit(solution)/shard_map/ppermute | solution.py:384
  47.6 13.7 %collective-permute-start.6 = (bf16[2,32,1536]{2,1,0:T(8,128)(2,1)}, bf16[2,32,1536]{2,1,0:T(8,128)(2,1)S(1)}, u32[]{:S(2)}, u32[]{:S(2)}) collective-permute-start(bf16[2,32,1536]{2,1,0:T(8,128)(2,1)} %get-tuple-element.31), channel_id=1, source_target_pairs={{0,7},{1,6},{2,1},{3,0},{4,3},{5,2},{6,5},{7,4},{8,15},{9,14},{10,... | collective-permute-start | bytes 589832 | tf_op jit(solution)/shard_map/ppermute | solution.py:384
  61.3 0.9 copy-start.8
  72.5 55.6 %all-to-all-start.1 = ((bf16[16,2,256,128]{3,2,1,0:T(8,128)(2,1)}), bf16[16,2,256,128]{3,2,1,0:T(8,128)(2,1)}, u32[]{:S(2)}, u32[]{:S(2)}) async-start(bf16[16,2,256,128]{3,2,1,0:T(8,128)(2,1)} %copy-done.5), calls=%async_computation.1 | async-start | bytes 4194304 | tf_op jit(solution)/shard_map/all_to_all | solution.py:391
  105.3 1.8 copy-start.12
  107.1 0.7 copy-start.14
  107.8 4.6 %copy-start.1 = (bf16[2,256,12288]{2,1,0:T(8,128)(2,1)S(1)}, bf16[2,256,12288]{2,1,0:T(8,128)(2,1)}, u32[]{:S(2)}) copy-start(bf16[2,256,12288]{2,1,0:T(8,128)(2,1)} %param.9) | copy-start | bytes 37748740
  112.4 2.8 %copy-start.2 = (bf16[12288,256]{1,0:T(8,128)(2,1)S(1)}, bf16[12288,256]{1,0:T(8,128)(2,1)}, u32[]{:S(2)}) copy-start(bf16[12288,256]{1,0:T(8,128)(2,1)} %all-gather.2.cloned.1.call-done.w_ref) | copy-start | bytes 18874372
  115.1 0.9 copy-start.7
  116.1 5.0 %copy-start.13 = (f32[2,2,144,1536]{3,2,1,0:T(8,128)S(1)}, f32[2,2,144,1536]{3,2,1,0:T(8,128)}, u32[]{:S(2)}) copy-start(f32[2,2,144,1536]{3,2,1,0:T(8,128)} %copy-done.12) | copy-start | bytes 10616836
  116.1 5.0 %copy-start.15 = (f32[2,2,8,1536]{3,2,1,0:T(8,128)S(1)}, f32[2,2,8,1536]{3,2,1,0:T(8,128)}, u32[]{:S(2)}) copy-start(f32[2,2,8,1536]{3,2,1,0:T(8,128)} %copy-done.14) | copy-start | bytes 589828
  126.3 1.8 copy-start.10
  128.1 2.0 %copy-start.11 = (f32[2,2,144,1536]{3,2,1,0:T(8,128)S(1)}, f32[2,2,144,1536]{3,2,1,0:T(8,128)}, u32[]{:S(2)}) copy-start(f32[2,2,144,1536]{3,2,1,0:T(8,128)} %copy-done.10) | copy-start | bytes 10616836
Sparse Core Ops, SparseCore 0:
  9.5 96.0 all-gather.1

commit v3 on v2

v3 whole, which is shorter than its diff:
```python
import functools
import math

import jax
import jax.numpy as jnp
from jax import lax
from jax.experimental import pallas as pl
from jax.experimental.pallas import tpu as pltpu
from jax.sharding import PartitionSpec as P

rope_base = 1000000.0
low = -1e30


def rope_tables(positions, width):
    half_width = width // 2
    exponent = jnp.arange(half_width, dtype=jnp.float32) * (2.0 / width)
    frequency = jnp.power(jnp.float32(rope_base), -exponent)
    angle = positions.astype(jnp.float32)[..., None] * frequency
    cosine = jnp.cos(angle)
    sine = jnp.sin(angle)
    return (
        jnp.concatenate([cosine, cosine], axis=-1),
        jnp.concatenate([-sine, sine], axis=-1),
    )


def rotate(values, cosine, signed_sine):
    swapped = pltpu.roll(values, values.shape[-1] // 2, 1)
    return values * cosine + swapped * signed_sine


def whole(shape):
    return pl.BlockSpec(shape, lambda *_: (0,) * len(shape))


def head_partner(me, step, count, sign):
    ring = count // 2
    turn = lax.rem(me // 2 + sign * (step // 2) + ring, ring)
    return 2 * turn + lax.rem(lax.rem(me, 2) + lax.rem(step, 2), 2)


def split_kernel(x_ref, *o_refs):
    me = lax.axis_index("head")
    part = o_refs[0].shape[2]
    for step, o_ref in enumerate(o_refs):
        to = head_partner(me, step, len(o_refs), 1)
        o_ref[...] = x_ref[:, :, pl.ds(pl.multiple_of(to * part, part), part)]


def split_columns(x, pieces):
    lead, rows, width = x.shape
    out = jax.ShapeDtypeStruct((lead, rows, width // pieces), x.dtype)
    return pl.pallas_call(split_kernel, out_shape=[out] * pieces, name="split_columns")(x)


def assemble_kernel(*refs):
    pieces = refs[:-2]
    o_ref, staged = refs[-2:]
    me = lax.axis_index("head")
    for step, piece in enumerate(pieces):
        staged[head_partner(me, step, len(pieces), -1)] = piece[...]
    queries_dev, recompute, double, all_rows = o_ref.shape
    head_dim = double // 2
    sources, _, rows, part = staged.shape
    per_tile = sources // recompute
    tile_len = per_tile * rows
    marker = (lax.broadcasted_iota(jnp.int32, (head_dim, all_rows), 0) == 0).astype(jnp.bfloat16)
    for i in range(queries_dev):
        for j in range(recompute):
            tile = staged[j * per_tile : (j + 1) * per_tile, i].reshape(tile_len, part)
            for g in range(part // head_dim):
                o_ref[i, j, :head_dim, g * tile_len : (g + 1) * tile_len] = tile[
                    :, g * head_dim : (g + 1) * head_dim
                ].T
            o_ref[i, j, head_dim:, :] = marker


def assemble(pieces, recompute, head_dim):
    queries_dev, rows, part = pieces[0].shape
    all_rows = len(pieces) // recompute * rows * (part // head_dim)
    return pl.pallas_call(
        assemble_kernel,
        out_shape=jax.ShapeDtypeStruct((queries_dev, recompute, 2 * head_dim, all_rows), pieces[0].dtype),
        scratch_shapes=[pltpu.VMEM((len(pieces),) + pieces[0].shape, pieces[0].dtype)],
        compiler_params=pltpu.CompilerParams(vmem_limit_bytes=20 * 2**20),
        name="assemble",
    )(*pieces)


def join_kernel(x_ref, o_ref):
    part = x_ref.shape[3]
    for j in range(x_ref.shape[0]):
        o_ref[:, :, j * part : (j + 1) * part] = x_ref[j]


def join_columns(x):
    pieces, lead, rows, part = x.shape
    return pl.pallas_call(
        join_kernel,
        out_shape=jax.ShapeDtypeStruct((lead, rows, pieces * part), x.dtype),
        name="join_columns",
    )(x)


def pick_kernel(rows_ref, keys_ref, values_ref, *o_refs):
    def step(d, carry):
        row = rows_ref[d]
        start = 0
        for o_ref in o_refs:
            at = slice(start, start + o_ref.shape[2])
            o_ref[d, 0] = keys_ref[row, 0, at]
            o_ref[d, 1] = values_ref[row, 0, at]
            start = at.stop
        return carry

    lax.fori_loop(0, o_refs[0].shape[0], step, 0)


def pick_spans(rows, keys, values, pieces):
    count = rows.shape[0]
    span_len, head_dim = keys.shape[2:]
    out = jax.ShapeDtypeStruct((count, 2, span_len // pieces, head_dim), keys.dtype)
    return pl.pallas_call(
        pick_kernel,
        in_specs=[
            pl.BlockSpec(memory_space=pltpu.SMEM),
            pl.BlockSpec(memory_space=pltpu.VMEM),
            pl.BlockSpec(memory_space=pltpu.VMEM),
        ],
        out_specs=[pl.BlockSpec(memory_space=pltpu.VMEM)] * pieces,
        out_shape=[out] * pieces,
        compiler_params=pltpu.CompilerParams(vmem_limit_bytes=20 * 2**20),
        name="pick_spans",
    )(rows, keys, values)


def blend(scores, before, exp_scale):
    after = jnp.maximum(before, jnp.max(scores, axis=0, keepdims=True))
    weights = jnp.exp2((scores - after) * exp_scale).astype(jnp.bfloat16)
    fade = jnp.exp2((before - after) * exp_scale)
    return after, weights, fade


def add_keys(exp_scale, q_ref, acc_ref, top_ref, where, keys, values, bias, wide):
    i, j = where
    all_rows = q_ref.shape[3]
    depth = keys.shape[1]
    ones = jnp.ones((acc_ref.shape[2] - values.shape[1], keys.shape[0]), jnp.bfloat16)
    values = jnp.concatenate([values.T, ones], axis=0)
    blocks = [pl.ds(start, wide) for start in range(0, all_rows, wide)]
    scores = {}
    for turn in range(-1, len(blocks)):
        if turn + 1 < len(blocks):
            scores[turn + 1] = jnp.dot(
                keys, q_ref[i, j, :depth, blocks[turn + 1]], preferred_element_type=jnp.float32
            )
        if turn >= 0:
            at = blocks[turn]
            now = scores.pop(turn)
            if bias is not None:
                now = now + bias
            after, weights, fade = blend(now, top_ref[i, j, :1, at], exp_scale)
            top_ref[i, j, :1, at] = after
            acc_ref[i, j, :, at] = acc_ref[i, j, :, at] * fade + jnp.dot(
                values, weights, preferred_element_type=jnp.float32
            )


def attend_kernel(exp_scale, tile_len, piece, pieces, last, *refs):
    refs = list(refs)
    owner_ref, tile_ref, q_ref, got_ref, cos_ref, sin_ref = refs[:6]
    del refs[:6]
    if last:
        acc_in, top_in, x_ref, w_ref, fresh_cos_ref, fresh_sin_ref, o_ref = refs[:7]
        del refs[:7]
    else:
        acc_out, top_out = refs[:2]
        del refs[:2]
    q_all, held, acc_ref, top_ref, q_sems, span_sems, state_sems = refs[:7]
    if last:
        x_held, w_held, total, x_sems = refs[7:]
    queries_dev, recompute, double, all_rows = q_all.shape
    slots, _, part_len, head_dim = held.shape[1:]
    wide = 4 * tile_len
    per_part = part_len // tile_len
    per_span = per_part * pieces

    def q_copy(i):
        return pltpu.make_async_copy(q_ref.at[i], q_all.at[i], q_sems.at[i])

    def span_copy(i, p):
        return pltpu.make_async_copy(
            got_ref.at[owner_ref[i, p]], held.at[i, p], span_sems.at[i, p]
        )

    def state_copies(i):
        pairs = [(acc_in, acc_ref), (top_in, top_ref)] if last else [(acc_ref, acc_out), (top_ref, top_out)]
        return [
            pltpu.make_async_copy(a.at[i], b.at[i], state_sems.at[i, k]) for k, (a, b) in enumerate(pairs)
        ]

    for i in range(queries_dev):
        q_copy(i).start()
        for p in range(slots):
            span_copy(i, p).start()
        if last:
            for copy in state_copies(i):
                copy.start()
    if last:
        steps = x_sems.shape[0]
        depth = x_held.shape[1] // steps
        copies = []
        for s in range(steps):
            at = pl.ds(s * depth, depth)
            copies.append(pltpu.make_async_copy(x_ref.at[:, at], x_held.at[:, at], x_sems.at[s, 0]))
            copies.append(pltpu.make_async_copy(w_ref.at[at, :], w_held.at[at, :], x_sems.at[s, 1]))
        for copy in copies:
            copy.start()
    key_lane = lax.broadcasted_iota(jnp.int32, (part_len, head_dim), 1)
    key_row = lax.broadcasted_iota(jnp.int32, (part_len, head_dim), 0)
    for i in range(queries_dev):
        if last:
            for copy in state_copies(i):
                copy.wait()
        else:
            top_ref[i] = jnp.full(top_ref.shape[1:], low, jnp.float32)
            acc_ref[i] = jnp.zeros(acc_ref.shape[1:], jnp.float32)
        q_copy(i).wait()

        def step(n, carry, i=i):
            group = n // recompute
            j = lax.rem(n, recompute)
            own = tile_ref[i, j]
            other = tile_ref[i, recompute - 1 - j]

            @pl.when(j == 0)
            def _():
                for inner in range(pieces):
                    span_copy(i, group * pieces + inner).wait()

            @pl.when(group * pieces * per_span + piece * per_part < own)
            def _():
                key_parts = []
                value_parts = []
                for inner in range(pieces):
                    p = group * pieces + inner
                    turned = rotate(
                        held[i, p, 0].astype(jnp.float32),
                        cos_ref[pl.ds(p, 1), :],
                        sin_ref[pl.ds(p, 1), :],
                    ).astype(jnp.bfloat16)
                    key_tile = p * per_span + piece * per_part + key_row // tile_len
                    hidden = (key_lane == 0) & ((key_tile >= own) | (key_tile == other))
                    key_parts.append(
                        jnp.concatenate(
                            [turned, jnp.where(hidden, low, 0.0).astype(jnp.bfloat16)], axis=1
                        )
                    )
                    value_parts.append(held[i, p, 1])
                add_keys(
                    exp_scale,
                    q_all,
                    acc_ref,
                    top_ref,
                    (i, j),
                    jnp.concatenate(key_parts, axis=0),
                    jnp.concatenate(value_parts, axis=0),
                    None,
                    wide,
                )

            return carry

        lax.fori_loop(0, slots // pieces * recompute, step, 0)
        if not last:
            for copy in state_copies(i):
                copy.start()
    if not last:
        for i in range(queries_dev):
            for copy in state_copies(i):
                copy.wait()
        return
    for copy in copies:
        copy.wait()
    total[...] = jnp.dot(x_held[:, :depth], w_held[:depth, :], preferred_element_type=jnp.float32)
    for s in range(1, steps):
        at = pl.ds(s * depth, depth)
        total[...] += jnp.dot(x_held[:, at], w_held[at, :], preferred_element_type=jnp.float32)
    fresh_keys = rotate(total[:, :head_dim], fresh_cos_ref[...], fresh_sin_ref[...]).astype(jnp.bfloat16)
    fresh_values = total[:, head_dim:].astype(jnp.bfloat16)
    rows = recompute * tile_len
    per_tile = o_ref.shape[0] // recompute
    key = lax.broadcasted_iota(jnp.int32, (rows, tile_len), 0)
    row = lax.broadcasted_iota(jnp.int32, (rows, tile_len), 1)
    for i in range(queries_dev):
        for j in range(recompute):
            own = tile_ref[i, j]
            other = tile_ref[i, recompute - 1 - j]
            in_own = key // tile_len == j
            allowed = (in_own & (key % tile_len <= row)) | (jnp.logical_not(in_own) & (other < own))
            bias = jnp.concatenate([jnp.where(allowed, 0.0, low)] * (wide // tile_len), axis=1)
            at_rows = slice(i * rows, (i + 1) * rows)
            add_keys(
                exp_scale, q_all, acc_ref, top_ref, (i, j), fresh_keys[at_rows], fresh_values[at_rows], bias, wide
            )
            for start in range(0, all_rows, wide):
                at = pl.ds(start, wide)
                result = acc_ref[i, j, :head_dim, at] / acc_ref[i, j, head_dim : head_dim + 1, at]
                result = result.astype(jnp.bfloat16).T
                for h in range(0, wide, tile_len):
                    column = (start + h) // tile_len * head_dim
                    o_ref[j * per_tile : (j + 1) * per_tile, i, :, column : column + head_dim] = result[
                        h : h + tile_len
                    ].reshape(per_tile, o_ref.shape[2], head_dim)


def attend(owner, tile_ids, queries, got, turn, exp_scale, tile_len, sources, piece, pieces, state=None, fresh=None):
    queries_dev, recompute, double, all_rows = queries.shape
    head_dim = double // 2
    slots = owner.shape[1]
    last = state is not None
    vmem = pl.BlockSpec(memory_space=pltpu.VMEM)
    smem = pl.BlockSpec(memory_space=pltpu.SMEM)
    hbm = pl.BlockSpec(memory_space=pltpu.HBM)
    shapes = [
        (queries_dev, recompute, head_dim + 16, all_rows),
        (queries_dev, recompute, 8, all_rows),
    ]
    args = [owner, tile_ids, queries, got] + turn
    specs = [smem, smem, hbm, hbm, vmem, vmem]
    if last:
        args += state + fresh
        specs += [hbm, hbm, hbm, hbm, vmem, vmem]
        rows = recompute * tile_len // sources
        part = all_rows // tile_len * head_dim
        out_shape = jax.ShapeDtypeStruct((sources, queries_dev, rows, part), queries.dtype)
        out_specs = vmem
        x, weights = fresh[:2]
        extra = [
            pltpu.VMEM(x.shape, x.dtype),
            pltpu.VMEM(weights.shape, weights.dtype),
            pltpu.VMEM((x.shape[0], weights.shape[1]), jnp.float32),
            pltpu.SemaphoreType.DMA((4, 2)),
        ]
    else:
        out_shape = [jax.ShapeDtypeStruct(shape, jnp.float32) for shape in shapes]
        out_specs = [hbm] * 2
        extra = []
    return pl.pallas_call(
        functools.partial(attend_kernel, exp_scale, tile_len, piece, pieces, last),
        in_specs=specs,
        out_specs=out_specs,
        out_shape=out_shape,
        scratch_shapes=[
            pltpu.VMEM(queries.shape, queries.dtype),
            pltpu.VMEM((queries_dev, slots) + got.shape[1:], got.dtype),
            pltpu.VMEM(shapes[0], jnp.float32),
            pltpu.VMEM(shapes[1], jnp.float32),
            pltpu.SemaphoreType.DMA((queries_dev,)),
            pltpu.SemaphoreType.DMA((queries_dev, slots)),
            pltpu.SemaphoreType.DMA((queries_dev, 2)),
        ]
        + extra,
        compiler_params=pltpu.CompilerParams(vmem_limit_bytes=(50 if last else 32) * 2**20),
        cost_estimate=pl.CostEstimate(
            flops=16 * 10**9 // pieces,
            bytes_accessed=12 * 10**6,
            transcendentals=16 * 10**6 // pieces,
        ),
        name="attend_last" if last else "attend_first",
    )(*args)


def body(
    tile_inputs,
    tile_queries,
    key_weight,
    value_weight,
    span_keys,
    span_values,
    span_slot,
    retrieval,
    tile_ids,
):
    queries_dev, tile_rows, width = tile_inputs.shape
    per_store, _, span_len, head_dim = span_keys.shape
    slot_count = retrieval.shape[1]
    recompute = tile_ids.shape[1]
    tile_len = tile_rows // recompute
    store_count = lax.axis_size("store")
    head_count = lax.axis_size("head")
    side = math.isqrt(store_count)
    exp_scale = head_dim ** (-0.5) * math.log2(math.e)

    store_rows = span_slot[retrieval]
    owners = store_rows // per_store
    hit = owners.reshape(1, -1) == jnp.arange(store_count, dtype=jnp.int32)[:, None]
    wanted = jnp.max(jnp.where(hit, (store_rows % per_store).reshape(1, -1), 0), axis=1)
    incoming = lax.all_to_all(
        wanted.reshape(store_count, 1), "store", split_axis=0, concat_axis=0, tiled=True
    )
    weights = lax.all_gather(
        jnp.concatenate([key_weight, value_weight], axis=1), "store", axis=0, tiled=True
    )
    pieces = 2
    picked = pick_spans(incoming.reshape(-1), span_keys, span_values, pieces)
    split = split_columns(tile_queries, head_count)
    ring = head_count // 2
    received = [split[0]]
    for step in range(1, head_count):
        pairs = [
            (me, 2 * ((me // 2 + step // 2) % ring) + (me + step) % 2) for me in range(head_count)
        ]
        received.append(lax.ppermute(split[step], "head", pairs))
    queries = assemble(received, recompute, head_dim)

    got = []
    for part in picked:
        if got:
            part, queries = lax.optimization_barrier((part, queries))
        got.append(lax.all_to_all(part, "store", split_axis=0, concat_axis=0, tiled=True))

    offsets = jnp.arange(tile_len, dtype=jnp.int32)
    positions = (tile_ids[:, :, None] * tile_len + offsets).reshape(-1)
    fresh_cos, fresh_sin = rope_tables(positions, head_dim)
    slot_cos, slot_sin = rope_tables(jnp.arange(slot_count, dtype=jnp.int32) * span_len, head_dim)

    fresh = [tile_inputs.reshape(queries_dev * tile_rows, width), weights, fresh_cos, fresh_sin]
    run = functools.partial(attend, owners, tile_ids, queries)
    turn = [slot_cos, slot_sin]
    state = run(got[0], turn, exp_scale, tile_len, head_count, 0, pieces)
    mixed = run(got[1], turn, exp_scale, tile_len, head_count, 1, pieces, list(state), fresh)
    return join_columns(
        lax.all_to_all(mixed, "head", split_axis=0, concat_axis=0, tiled=True)
    )


def solution(mesh):
    placed = (
        P("store", None, None),
        P("store", "head", None),
        P("store", "head"),
        P("store", "head"),
        P("store", "head", None, None),
        P("store", "head", None, None),
        P(),
        P("store", None),
        P("store", None),
    )
    return jax.shard_map(
        body, mesh=mesh, in_specs=placed, out_specs=P("store", "head", None), check_vma=False
    )
```

time: 186 us -> 177 us (0.952)
  the two profiles are of different devices: /device:TPU:4 before, /device:TPU:102 now
where the time goes in v3:
time: 177 us; the launch traced here: 179 us
  Pallas kernels  63 us (36%)
  blocking collectives  37.1 us (21%)
  starting transfers between devices  25.9 us (15%)
  waiting for transfers between devices  23.4 us (13%)
  between operations  13.5 us (8%)
  local copies, waits for them, and re-layouts  10.6 us (6%)
  other arithmetic  5.33 us (3%)
    pallas_call x2, Pallas kernels, attend(): pl.pallas_call(functools.partial(attend_kernel, exp_scale, tile_len, piec...  56 us
    all_to_all x1, blocking collectives, body(): lax.all_to_all(mixed, 'head', split_axis=0, concat_axis=0, tiled=True)  26.4 us
    all_to_all x2, starting transfers between devices, body(): lax.all_to_all(part, 'store', split_axis=0, concat_axis=0, tiled=True)  17.2 us
    ppermute x7, waiting for transfers between devices, body(): received.append(lax.ppermute(split[step], 'head', pairs))  14.1 us
    all_to_all x1, blocking collectives, body(): lax.all_to_all(wanted.reshape(store_count, 1), 'store', split_axis=0, con...  10.8 us
    unnamed x24, local copies, waits for them, and re-layouts  9.64 us
    all_to_all x2, waiting for transfers between devices, body(): lax.all_to_all(part, 'store', split_axis=0, concat_axis=0, tiled=True)  9.24 us
    ppermute x7, starting transfers between devices, body(): received.append(lax.ppermute(split[step], 'head', pairs))  8.66 us
  transfers between devices with their start and end apart: 10, of which 6 were waited for; matrix products, arithmetic and copies ran while one was open for 2% of the time, Pallas kernels for 15%

profile of v3, /device:TPU:102, one launch (start us, length us, event | category | flops | bytes accessed | tf_op | source)
XLA Modules:
  0.0 178.7 jit_solution(10237593594837570354)
XLA Ops:
  6.5 2.0 %pad_maximum_fusion = bf16[768,256]{1,0:T(8,128)(2,1)} fusion(bf16[768,128]{1,0:T(8,128)(2,1)} %param.12, bf16[768,128]{1,0:T(8,128)(2,1)} %param.11), kind=kLoop, calls=%fused_computation.1 | loop fusion | flops 786432 | bytes 786432 | tf_op jit(solution)/shard_map/concatenate | solution.py:404
  8.5 0.7 compare_select_fusion
  10.2 10.8 %all_to_all.24 = s32[16,1,1]{2,1,0:T(1,128)S(1)} all-to-all(s32[16,1,1]{2,1,0:T(1,128)S(1)} %copy.12), channel_id=1, replica_groups=mesh['store'=16,'head'=8] {'store'}, dimensions={0} | all-to-all | bytes 128 | tf_op jit(solution)/shard_map/all_to_all | solution.py:400
  21.4 1.7 copy-done.4
  23.0 0.9 pick_spans.1
  24.0 1.3 copy-done.5
  25.3 1.3 copy-done.6
  26.6 7.7 %all-to-all-start.2 = ((bf16[16,2,256,128]{3,2,1,0:T(8,128)(2,1)}), bf16[16,2,256,128]{3,2,1,0:T(8,128)(2,1)}, u32[]{:S(2)}, u32[]{:S(2)}) async-start(bf16[16,2,256,128]{3,2,1,0:T(8,128)(2,1)} %copy-done.6), calls=%async_computation.2 | async-start | bytes 4194304 | tf_op jit(solution)/shard_map/all_to_all | solution.py:422
  34.3 2.7 %split_columns.1 = (bf16[2,32,1536]{2,1,0:T(8,128)(2,1)}, bf16[2,32,1536]{2,1,0:T(8,128)(2,1)}, bf16[2,32,1536]{2,1,0:T(8,128)(2,1)}, bf16[2,32,1536]{2,1,0:T(8,...) custom-call(bf16[2,32,12288]{2,1,0:T(8,128)(2,1)} %x_ref.1), custom_call_target="tpu_custom_call" | custom-call | tf_op jit(solution)/shard_map/split_columns/pallas_call | solution.py:54
  37.0 1.6 collective-permute-start.1
  38.6 1.4 collective-permute-start.2
  40.0 1.6 collective-permute-start.3
  41.6 1.5 collective-permute-start.4
  43.1 1.7 collective-permute-start.5
  44.8 1.3 collective-permute-done.1.refs_2_
  46.1 0.9 collective-permute-start.6
  47.0 2.7 %collective-permute-done.2.refs_3_ = bf16[2,32,1536]{2,1,0:T(8,128)(2,1)S(1)} collective-permute-done((bf16[2,32,1536]{2,1,0:T(8,128)(2,1)}, bf16[2,32,1536]{2,1,0:T(8,128)(2,1)S(1)}, u32[]{:S(2)}, u32[]{:S(2)}) %collective-permute-start.2) | collective-permute-done | bytes 196640 | tf_op jit(solution)/shard_map/ppermute | solution.py:415
  49.7 6.1 %collective-permute-done.3.refs_4_ = bf16[2,32,1536]{2,1,0:T(8,128)(2,1)S(1)} collective-permute-done((bf16[2,32,1536]{2,1,0:T(8,128)(2,1)}, bf16[2,32,1536]{2,1,0:T(8,128)(2,1)S(1)}, u32[]{:S(2)}, u32[]{:S(2)}) %collective-permute-start.3) | collective-permute-done | bytes 196640 | tf_op jit(solution)/shard_map/ppermute | solution.py:415
  55.8 3.4 %collective-permute-done.4.refs_5_ = bf16[2,32,1536]{2,1,0:T(8,128)(2,1)S(1)} collective-permute-done((bf16[2,32,1536]{2,1,0:T(8,128)(2,1)}, bf16[2,32,1536]{2,1,0:T(8,128)(2,1)S(1)}, u32[]{:S(2)}, u32[]{:S(2)}) %collective-permute-start.4) | collective-permute-done | bytes 196640 | tf_op jit(solution)/shard_map/ppermute | solution.py:415
  59.8 0.9 copy-done.10
  61.4 9.2 %all-to-all-done.2.refs_3_ = bf16[16,2,256,128]{3,2,1,0:T(8,128)(2,1)} async-done(((bf16[16,2,256,128]{3,2,1,0:T(8,128)(2,1)}), bf16[16,2,256,128]{3,2,1,0:T(8,128)(2,1)}, u32[]{:S(2)}, u32[]{:S(2)}) %all-to-all-start.2) | async-done | bytes 2097184 | tf_op jit(solution)/shard_map/all_to_all | solution.py:422
  70.7 9.5 %all-to-all-start.1 = ((bf16[16,2,256,128]{3,2,1,0:T(8,128)(2,1)}), bf16[16,2,256,128]{3,2,1,0:T(8,128)(2,1)}, u32[]{:S(2)}, u32[]{:S(2)}) async-start(bf16[16,2,256,128]{3,2,1,0:T(8,128)(2,1)} %copy-done.5), calls=%async_computation.1 | async-start | bytes 4194304 | tf_op jit(solution)/shard_map/all_to_all | solution.py:422
  80.5 1.0 fusion
  81.5 0.9 pad_maximum_fusion.1
  82.4 23.0 %attend_first.1 = (f32[2,2,144,1536]{3,2,1,0:T(8,128)S(1)}, f32[2,2,8,1536]{3,2,1,0:T(8,128)S(1)}) custom-call(s32[2,8]{1,0:T(2,128)S(1)} %and_select_fusion.2.refs_0_, s32[2,2]{1,0:T(2,128)S(1)} %copy-done.11, bf16[2,2,256,1536]{3,2,1,0:T(8,128)(2,1)S(1)} %assemble.1.refs_2_, bf16[16,2,256,128]{3,2,1,0:T(8,128)(2,1)} %all-to-all-done.2.refs_3_, ...), custom_call_target="tpu_custom_call" | custom-call | flops 8000000000 | bytes 12000000 | tf_op jit(solution)/shard_map/attend_first/pallas_call | solution.py:350
  105.4 1.8 %copy-done.2 = f32[2,2,144,1536]{3,2,1,0:T(8,128)} copy-done((f32[2,2,144,1536]{3,2,1,0:T(8,128)}, f32[2,2,144,1536]{3,2,1,0:T(8,128)S(1)}, u32[]{:S(2)}) %copy-start.2) | copy-done | bytes 3538968
  107.2 0.7 copy-done.8
  107.9 0.9 copy-done.7
  108.9 0.9 copy-done.9
  109.8 33.0 %attend_last.1 = bf16[8,2,32,1536]{3,2,1,0:T(8,128)(2,1)S(1)} custom-call(s32[2,8]{1,0:T(2,128)S(1)} %and_select_fusion.2.refs_0_, s32[2,2]{1,0:T(2,128)S(1)} %copy-done.11, bf16[2,2,256,1536]{3,2,1,0:T(8,128)(2,1)} %copy-done.1, bf16[16,2,256,128]{3,2,1,0:T(8,128)(2,1)} %all-to-all-done.1.refs_3_, f32[8,128]{1,0:T(8,128)S(1)} %get-tuple-element.41.refs_4_, ...), custom_call_target="tpu_custom_call" | custom-call | flops 8000000000 | bytes 12000000 | tf_op jit(solution)/shard_map/attend_last/pallas_call | solution.py:350
  142.9 26.4 %all_to_all.25.x_ref = bf16[8,2,32,1536]{3,2,1,0:T(8,128)(2,1)} all-to-all(bf16[8,2,32,1536]{3,2,1,0:T(8,128)(2,1)S(1)} %attend_last.1), channel_id=1, replica_groups=mesh['store'=16,'head'=8] {'head'}, dimensions={0} | all-to-all | bytes 3145728 | tf_op jit(solution)/shard_map/all_to_all | solution.py:435
  169.2 2.7 %join_columns.1 = bf16[2,32,12288]{2,1,0:T(8,128)(2,1)} custom-call(bf16[8,2,32,1536]{3,2,1,0:T(8,128)(2,1)} %all_to_all.25.x_ref), custom_call_target="tpu_custom_call" | custom-call | tf_op jit(solution)/shard_map/join_columns/pallas_call | solution.py:99
  (40 shorter events, 3.0 us)
Async XLA Ops:
  6.5 2.8 %copy-start = (s32[256]{0:T(256)S(1)}, s32[256]{0:T(256)}, u32[]{:S(2)}) copy-start(s32[256]{0:T(256)} %param.15) | copy-start | bytes 3076
  6.5 14.8 %copy-start.3 = (bf16[16,1,512,128]{3,2,1,0:T(8,128)(2,1)S(1)}, bf16[16,1,512,128]{3,2,1,0:T(8,128)(2,1)}, u32[]{:S(2)}) copy-start(bf16[16,1,512,128]{3,2,1,0:T(8,128)(2,1)} %keys_ref.1) | copy-start | bytes 6291460
  6.5 101.4 %all-gather.2.cloned.1.call-start = ((), (), s32[]{:S(2)}) async-start(), calls=%async_computation.4 | async-start | bytes 6684672 | tf_op jit(solution)/shard_map/all_gather | solution.py:403
  21.3 1.7 copy-start.4
  23.9 1.3 copy-start.5
  25.3 1.3 copy-start.6
  26.6 44.1 %all-to-all-start.2 = ((bf16[16,2,256,128]{3,2,1,0:T(8,128)(2,1)}), bf16[16,2,256,128]{3,2,1,0:T(8,128)(2,1)}, u32[]{:S(2)}, u32[]{:S(2)}) async-start(bf16[16,2,256,128]{3,2,1,0:T(8,128)(2,1)} %copy-done.6), calls=%async_computation.2 | async-start | bytes 4194304 | tf_op jit(solution)/shard_map/all_to_all | solution.py:422
  37.0 6.1 %collective-permute-start = (bf16[2,32,1536]{2,1,0:T(8,128)(2,1)}, bf16[2,32,1536]{2,1,0:T(8,128)(2,1)S(1)}, u32[]{:S(2)}, u32[]{:S(2)}) collective-permute-start(bf16[2,32,1536]{2,1,0:T(8,128)(2,1)} %get-tuple-element.21), channel_id=1, source_target_pairs={{0,1},{1,0},{2,3},{3,2},{4,5},{5,4},{6,7},{7,6},{8,9},{9,8},{10,11... | collective-permute-start | bytes 589832 | tf_op jit(solution)/shard_map/ppermute | solution.py:415
  37.0 9.1 %collective-permute-start.1 = (bf16[2,32,1536]{2,1,0:T(8,128)(2,1)}, bf16[2,32,1536]{2,1,0:T(8,128)(2,1)S(1)}, u32[]{:S(2)}, u32[]{:S(2)}) collective-permute-start(bf16[2,32,1536]{2,1,0:T(8,128)(2,1)} %get-tuple-element.22), channel_id=1, source_target_pairs={{0,2},{1,3},{2,4},{3,5},{4,6},{5,7},{6,0},{7,1},{8,10},{9,11},{10,... | collective-permute-start | bytes 589832 | tf_op jit(solution)/shard_map/ppermute | solution.py:415
  38.6 11.1 %collective-permute-start.2 = (bf16[2,32,1536]{2,1,0:T(8,128)(2,1)}, bf16[2,32,1536]{2,1,0:T(8,128)(2,1)S(1)}, u32[]{:S(2)}, u32[]{:S(2)}) collective-permute-start(bf16[2,32,1536]{2,1,0:T(8,128)(2,1)} %get-tuple-element.23), channel_id=1, source_target_pairs={{0,3},{1,2},{2,5},{3,4},{4,7},{5,6},{6,1},{7,0},{8,11},{9,10},{10,... | collective-permute-start | bytes 589832 | tf_op jit(solution)/shard_map/ppermute | solution.py:415
  40.0 15.8 %collective-permute-start.3 = (bf16[2,32,1536]{2,1,0:T(8,128)(2,1)}, bf16[2,32,1536]{2,1,0:T(8,128)(2,1)S(1)}, u32[]{:S(2)}, u32[]{:S(2)}) collective-permute-start(bf16[2,32,1536]{2,1,0:T(8,128)(2,1)} %get-tuple-element.24), channel_id=1, source_target_pairs={{0,4},{1,5},{2,6},{3,7},{4,0},{5,1},{6,2},{7,3},{8,12},{9,13},{10,... | collective-permute-start | bytes 589832 | tf_op jit(solution)/shard_map/ppermute | solution.py:415
  41.6 17.6 %collective-permute-start.4 = (bf16[2,32,1536]{2,1,0:T(8,128)(2,1)}, bf16[2,32,1536]{2,1,0:T(8,128)(2,1)S(1)}, u32[]{:S(2)}, u32[]{:S(2)}) collective-permute-start(bf16[2,32,1536]{2,1,0:T(8,128)(2,1)} %get-tuple-element.25), channel_id=1, source_target_pairs={{0,5},{1,4},{2,7},{3,6},{4,1},{5,0},{6,3},{7,2},{8,13},{9,12},{10,... | collective-permute-start | bytes 589832 | tf_op jit(solution)/shard_map/ppermute | solution.py:415
  43.1 16.1 %collective-permute-start.5 = (bf16[2,32,1536]{2,1,0:T(8,128)(2,1)}, bf16[2,32,1536]{2,1,0:T(8,128)(2,1)S(1)}, u32[]{:S(2)}, u32[]{:S(2)}) collective-permute-start(bf16[2,32,1536]{2,1,0:T(8,128)(2,1)} %get-tuple-element.26), channel_id=1, source_target_pairs={{0,6},{1,7},{2,0},{3,1},{4,2},{5,3},{6,4},{7,5},{8,14},{9,15},{10,... | collective-permute-start | bytes 589832 | tf_op jit(solution)/shard_map/ppermute | solution.py:415
  46.1 13.7 %collective-permute-start.6 = (bf16[2,32,1536]{2,1,0:T(8,128)(2,1)}, bf16[2,32,1536]{2,1,0:T(8,128)(2,1)S(1)}, u32[]{:S(2)}, u32[]{:S(2)}) collective-permute-start(bf16[2,32,1536]{2,1,0:T(8,128)(2,1)} %get-tuple-element.27), channel_id=1, source_target_pairs={{0,7},{1,6},{2,1},{3,0},{4,3},{5,2},{6,5},{7,4},{8,15},{9,14},{10,... | collective-permute-start | bytes 589832 | tf_op jit(solution)/shard_map/ppermute | solution.py:415
  59.8 0.9 copy-start.10
  61.4 21.0 %copy-start.1 = (bf16[2,2,256,1536]{3,2,1,0:T(8,128)(2,1)}, bf16[2,2,256,1536]{3,2,1,0:T(8,128)(2,1)S(1)}, u32[]{:S(2)}) copy-start(bf16[2,2,256,1536]{3,2,1,0:T(8,128)(2,1)S(1)} %assemble.1.refs_2_) | copy-start | bytes 9437188
  61.4 19.0 %copy-start.11 = (s32[2,2]{1,0:T(2,128)S(1)}, s32[2,2]{1,0:T(2,128)}, u32[]{:S(2)}) copy-start(s32[2,2]{1,0:T(2,128)} %refs_1_.3) | copy-start | bytes 52
  70.7 37.3 %all-to-all-start.1 = ((bf16[16,2,256,128]{3,2,1,0:T(8,128)(2,1)}), bf16[16,2,256,128]{3,2,1,0:T(8,128)(2,1)}, u32[]{:S(2)}, u32[]{:S(2)}) async-start(bf16[16,2,256,128]{3,2,1,0:T(8,128)(2,1)} %copy-done.5), calls=%async_computation.1 | async-start | bytes 4194304 | tf_op jit(solution)/shard_map/all_to_all | solution.py:422
  105.4 1.8 %copy-start.2 = (f32[2,2,144,1536]{3,2,1,0:T(8,128)}, f32[2,2,144,1536]{3,2,1,0:T(8,128)S(1)}, u32[]{:S(2)}) copy-start(f32[2,2,144,1536]{3,2,1,0:T(8,128)S(1)} %get-tuple-element.31.refs_6_) | copy-start | bytes 10616836
  107.2 0.7 copy-start.8
  107.9 1.0 copy-start.7
  108.9 0.9 copy-start.9
Sparse Core Ops, SparseCore 0:
  9.5 90.8 all-gather.1

commit v4 on v3

--- a/solution.py
+++ b/solution.py
@@ -88,19 +88,45 @@
     )(*pieces)
 
 
-def join_kernel(x_ref, o_ref):
-    part = x_ref.shape[3]
-    for j in range(x_ref.shape[0]):
-        o_ref[:, :, j * part : (j + 1) * part] = x_ref[j]
-
-
-def join_columns(x):
-    pieces, lead, rows, part = x.shape
+def join_kernel(*refs):
+    pieces = refs[:-2]
+    o_ref, sems = refs[-2:]
+    me = lax.axis_index("head")
+    part = pieces[0].shape[2]
+    copies = []
+    for step, piece in enumerate(pieces):
+        at = head_partner(me, step, len(pieces), -1) * part
+        copies.append(
+            pltpu.make_async_copy(
+                piece, o_ref.at[:, :, pl.ds(pl.multiple_of(at, part), part)], sems.at[step]
+            )
+        )
+    for copy in copies:
+        copy.start()
+    for copy in copies:
+        copy.wait()
+
+
+def join_columns(pieces):
+    lead, rows, part = pieces[0].shape
     return pl.pallas_call(
         join_kernel,
-        out_shape=jax.ShapeDtypeStruct((lead, rows, pieces * part), x.dtype),
+        in_specs=[pl.BlockSpec(memory_space=pltpu.VMEM)] * len(pieces),
+        out_specs=pl.BlockSpec(memory_space=pltpu.HBM),
+        out_shape=jax.ShapeDtypeStruct((lead, rows, len(pieces) * part), pieces[0].dtype),
+        scratch_shapes=[pltpu.SemaphoreType.DMA((len(pieces),))],
         name="join_columns",
-    )(x)
+    )(*pieces)
+
+
+def head_exchange(pieces):
+    count = len(pieces)
+    ring = count // 2
+    received = [pieces[0]]
+    for step in range(1, count):
+        pairs = [(me, 2 * ((me // 2 + step // 2) % ring) + (me + step) % 2) for me in range(count)]
+        received.append(lax.ppermute(pieces[step], "head", pairs))
+    return received
 
 
 def pick_kernel(rows_ref, keys_ref, values_ref, *o_refs):
@@ -150,36 +176,40 @@
     values = jnp.concatenate([values.T, ones], axis=0)
     blocks = [pl.ds(start, wide) for start in range(0, all_rows, wide)]
     scores = {}
+    tops = {}
     for turn in range(-1, len(blocks)):
         if turn + 1 < len(blocks):
-            scores[turn + 1] = jnp.dot(
-                keys, q_ref[i, j, :depth, blocks[turn + 1]], preferred_element_type=jnp.float32
-            )
+            at = blocks[turn + 1]
+            now = jnp.dot(keys, q_ref[i, j, :depth, at], preferred_element_type=jnp.float32)
+            if bias is not None:
+                now = now + bias
+            scores[turn + 1] = now
+            tops[turn + 1] = jnp.max(now, axis=0, keepdims=True)
         if turn >= 0:
             at = blocks[turn]
-            now = scores.pop(turn)
-            if bias is not None:
-                now = now + bias
-            after, weights, fade = blend(now, top_ref[i, j, :1, at], exp_scale)
+            before = top_ref[i, j, :1, at]
+            after = jnp.maximum(before, tops.pop(turn))
+            weights = jnp.exp2((scores.pop(turn) - after) * exp_scale).astype(jnp.bfloat16)
+            fade = jnp.exp2((before - after) * exp_scale)
             top_ref[i, j, :1, at] = after
             acc_ref[i, j, :, at] = acc_ref[i, j, :, at] * fade + jnp.dot(
                 values, weights, preferred_element_type=jnp.float32
             )
 
 
-def attend_kernel(exp_scale, tile_len, piece, pieces, last, *refs):
+def attend_kernel(exp_scale, tile_len, piece, pieces, sources, last, *refs):
     refs = list(refs)
     owner_ref, tile_ref, q_ref, got_ref, cos_ref, sin_ref = refs[:6]
     del refs[:6]
     if last:
-        acc_in, top_in, x_ref, w_ref, fresh_cos_ref, fresh_sin_ref, o_ref = refs[:7]
-        del refs[:7]
+        state_ref, x_ref, w_ref, fresh_cos_ref, fresh_sin_ref = refs[:5]
+        o_refs = refs[5 : 5 + sources]
+        del refs[: 5 + sources]
     else:
-        acc_out, top_out = refs[:2]
-        del refs[:2]
+        state_ref = refs.pop(0)
     q_all, held, acc_ref, top_ref, q_sems, span_sems, state_sems = refs[:7]
     if last:
-        x_held, w_held, total, x_sems = refs[7:]
+        x_held, w_held, total, staged, x_sems = refs[7:]
     queries_dev, recompute, double, all_rows = q_all.shape
     slots, _, part_len, head_dim = held.shape[1:]
     wide = 4 * tile_len
@@ -195,9 +225,16 @@
         )
 
     def state_copies(i):
-        pairs = [(acc_in, acc_ref), (top_in, top_ref)] if last else [(acc_ref, acc_out), (top_ref, top_out)]
+        kept = acc_ref.shape[2] - top_ref.shape[2]
+        pairs = [
+            (acc_ref.at[i, :, :kept], state_ref.at[i, :, :kept]),
+            (top_ref.at[i], state_ref.at[i, :, kept:]),
+        ]
         return [
-            pltpu.make_async_copy(a.at[i], b.at[i], state_sems.at[i, k]) for k, (a, b) in enumerate(pairs)
+            pltpu.make_async_copy(b, a, state_sems.at[i, k])
+            if last
+            else pltpu.make_async_copy(a, b, state_sems.at[i, k])
+            for k, (a, b) in enumerate(pairs)
         ]
 
     for i in range(queries_dev):
@@ -239,11 +276,12 @@
                 for inner in range(pieces):
                     span_copy(i, group * pieces + inner).wait()
 
-            @pl.when(group * pieces * per_span + piece * per_part < own)
-            def _():
+            needed = own - group * pieces * per_span - piece * per_part
+
+            def add(count, i=i):
                 key_parts = []
                 value_parts = []
-                for inner in range(pieces):
+                for inner in range(count):
                     p = group * pieces + inner
                     turned = rotate(
                         held[i, p, 0].astype(jnp.float32),
@@ -270,6 +308,14 @@
                     wide,
                 )
 
+            @pl.when((needed > 0) & (needed <= per_span))
+            def _():
+                add(1)
+
+            @pl.when(needed > per_span)
+            def _():
+                add(2)
+
             return carry
 
         lax.fori_loop(0, slots // pieces * recompute, step, 0)
@@ -290,7 +336,7 @@
     fresh_keys = rotate(total[:, :head_dim], fresh_cos_ref[...], fresh_sin_ref[...]).astype(jnp.bfloat16)
     fresh_values = total[:, head_dim:].astype(jnp.bfloat16)
     rows = recompute * tile_len
-    per_tile = o_ref.shape[0] // recompute
+    per_tile = sources // recompute
     key = lax.broadcasted_iota(jnp.int32, (rows, tile_len), 0)
     row = lax.broadcasted_iota(jnp.int32, (rows, tile_len), 1)
     for i in range(queries_dev):
@@ -306,13 +352,16 @@
             )
             for start in range(0, all_rows, wide):
                 at = pl.ds(start, wide)
-                result = acc_ref[i, j, :head_dim, at] / acc_ref[i, j, head_dim : head_dim + 1, at]
+                result = acc_ref[i, j, :head_dim, at] * (1.0 / acc_ref[i, j, head_dim : head_dim + 1, at])
                 result = result.astype(jnp.bfloat16).T
                 for h in range(0, wide, tile_len):
                     column = (start + h) // tile_len * head_dim
-                    o_ref[j * per_tile : (j + 1) * per_tile, i, :, column : column + head_dim] = result[
+                    staged[j * per_tile : (j + 1) * per_tile, i, :, column : column + head_dim] = result[
                         h : h + tile_len
-                    ].reshape(per_tile, o_ref.shape[2], head_dim)
+                    ].reshape(per_tile, staged.shape[2], head_dim)
+    me = lax.axis_index("head")
+    for move, o_ref in enumerate(o_refs):
+        o_ref[...] = staged[head_partner(me, move, sources, 1)]
 
 
 def attend(owner, tile_ids, queries, got, turn, exp_scale, tile_len, sources, piece, pieces, state=None, fresh=None):
@@ -330,25 +379,26 @@
     args = [owner, tile_ids, queries, got] + turn
     specs = [smem, smem, hbm, hbm, vmem, vmem]
     if last:
-        args += state + fresh
-        specs += [hbm, hbm, hbm, hbm, vmem, vmem]
+        args += [state] + fresh
+        specs += [hbm, hbm, hbm, vmem, vmem]
         rows = recompute * tile_len // sources
         part = all_rows // tile_len * head_dim
-        out_shape = jax.ShapeDtypeStruct((sources, queries_dev, rows, part), queries.dtype)
-        out_specs = vmem
+        out_shape = [jax.ShapeDtypeStruct((queries_dev, rows, part), queries.dtype)] * sources
+        out_specs = [vmem] * sources
         x, weights = fresh[:2]
         extra = [
             pltpu.VMEM(x.shape, x.dtype),
             pltpu.VMEM(weights.shape, weights.dtype),
             pltpu.VMEM((x.shape[0], weights.shape[1]), jnp.float32),
+            pltpu.VMEM((sources, queries_dev, rows, part), queries.dtype),
             pltpu.SemaphoreType.DMA((4, 2)),
         ]
     else:
-        out_shape = [jax.ShapeDtypeStruct(shape, jnp.float32) for shape in shapes]
-        out_specs = [hbm] * 2
+        out_shape = jax.ShapeDtypeStruct(shapes[0], jnp.float32)
+        out_specs = hbm
         extra = []
     return pl.pallas_call(
-        functools.partial(attend_kernel, exp_scale, tile_len, piece, pieces, last),
+        functools.partial(attend_kernel, exp_scale, tile_len, piece, pieces, sources, last),
         in_specs=specs,
         out_specs=out_specs,
         out_shape=out_shape,
@@ -406,13 +456,7 @@
     pieces = 2
     picked = pick_spans(incoming.reshape(-1), span_keys, span_values, pieces)
     split = split_columns(tile_queries, head_count)
-    ring = head_count // 2
-    received = [split[0]]
-    for step in range(1, head_count):
-        pairs = [
-            (me, 2 * ((me // 2 + step // 2) % ring) + (me + step) % 2) for me in range(head_count)
-        ]
-        received.append(lax.ppermute(split[step], "head", pairs))
+    received = head_exchange(split)
     queries = assemble(received, recompute, head_dim)
 
     got = []
@@ -430,10 +474,8 @@
     run = functools.partial(attend, owners, tile_ids, queries)
     turn = [slot_cos, slot_sin]
     state = run(got[0], turn, exp_scale, tile_len, head_count, 0, pieces)
-    mixed = run(got[1], turn, exp_scale, tile_len, head_count, 1, pieces, list(state), fresh)
-    return join_columns(
-        lax.all_to_all(mixed, "head", split_axis=0, concat_axis=0, tiled=True)
-    )
+    mixed = run(got[1], turn, exp_scale, tile_len, head_count, 1, pieces, state, fresh)
+    return join_columns(head_exchange(mixed))
 
 
 def solution(mesh):

time: 177 us -> 174 us (0.983)
  the two profiles are of different devices: /device:TPU:102 before, /device:TPU:6 now
where the time goes in v4:
time: 174 us; the launch traced here: 172 us
  Pallas kernels  58 us (33%)
  waiting for transfers between devices  42.2 us (24%)
  starting transfers between devices  29.2 us (17%)
  blocking collectives  13.6 us (8%)
  between operations  13.6 us (8%)
  local copies, waits for them, and re-layouts  10.1 us (6%)
  other arithmetic  5.35 us (3%)
    pallas_call x2, Pallas kernels, attend(): pl.pallas_call(functools.partial(attend_kernel, exp_scale, tile_len, piec...  51.1 us
    ppermute x14, waiting for transfers between devices, head_exchange(): received.append(lax.ppermute(pieces[step], 'head', pairs))  25.5 us
    ppermute x14, starting transfers between devices, head_exchange(): received.append(lax.ppermute(pieces[step], 'head', pairs))  17 us
    all_to_all x2, waiting for transfers between devices, body(): lax.all_to_all(part, 'store', split_axis=0, concat_axis=0, tiled=True)  16.7 us
    all_to_all x1, blocking collectives, body(): lax.all_to_all(wanted.reshape(store_count, 1), 'store', split_axis=0, con...  13.6 us
    all_to_all x2, starting transfers between devices, body(): lax.all_to_all(part, 'store', split_axis=0, concat_axis=0, tiled=True)  12.1 us
    unnamed x36, local copies, waits for them, and re-layouts  9.23 us
  transfers between devices with their start and end apart: 17, of which 12 were waited for; matrix products, arithmetic and copies ran while one was open for 3% of the time, Pallas kernels for 14%

profile of v4, /device:TPU:6, one launch (start us, length us, event | category | flops | bytes accessed | tf_op | source)
XLA Modules:
  0.0 172.1 jit_solution(2480800879632535267)
XLA Ops:
  6.5 2.0 %pad_maximum_fusion = bf16[768,256]{1,0:T(8,128)(2,1)} fusion(bf16[768,128]{1,0:T(8,128)(2,1)} %param.12, bf16[768,128]{1,0:T(8,128)(2,1)} %param.11), kind=kLoop, calls=%fused_computation.1 | loop fusion | flops 786432 | bytes 786432 | tf_op jit(solution)/shard_map/concatenate | solution.py:454
  10.2 13.6 %all_to_all.19 = s32[16,1,1]{2,1,0:T(1,128)S(1)} all-to-all(s32[16,1,1]{2,1,0:T(1,128)S(1)} %copy.12), channel_id=1, replica_groups=mesh['store'=16,'head'=8] {'store'}, dimensions={0} | all-to-all | bytes 128 | tf_op jit(solution)/shard_map/all_to_all | solution.py:450
  24.2 1.6 copy-done.3
  26.7 1.3 copy-done.4
  28.0 1.3 copy-done.5
  29.3 6.3 %all-to-all-start.2 = ((bf16[16,2,256,128]{3,2,1,0:T(8,128)(2,1)}), bf16[16,2,256,128]{3,2,1,0:T(8,128)(2,1)}, u32[]{:S(2)}, u32[]{:S(2)}) async-start(bf16[16,2,256,128]{3,2,1,0:T(8,128)(2,1)} %copy-done.5), calls=%async_computation.2 | async-start | bytes 4194304 | tf_op jit(solution)/shard_map/all_to_all | solution.py:466
  35.6 2.7 %split_columns.1 = (bf16[2,32,1536]{2,1,0:T(8,128)(2,1)}, bf16[2,32,1536]{2,1,0:T(8,128)(2,1)}, bf16[2,32,1536]{2,1,0:T(8,128)(2,1)}, bf16[2,32,1536]{2,1,0:T(8,...) custom-call(bf16[2,32,12288]{2,1,0:T(8,128)(2,1)} %x_ref.1), custom_call_target="tpu_custom_call" | custom-call | tf_op jit(solution)/shard_map/split_columns/pallas_call | solution.py:54
  38.3 1.6 collective-permute-start.1
  39.9 1.4 collective-permute-start.2
  41.3 1.6 collective-permute-start.3
  42.9 1.5 collective-permute-start.4
  44.4 1.7 collective-permute-start.5
  46.1 1.3 collective-permute-done.1.refs_2_
  48.3 2.7 %collective-permute-done.2.refs_3_ = bf16[2,32,1536]{2,1,0:T(8,128)(2,1)S(1)} collective-permute-done((bf16[2,32,1536]{2,1,0:T(8,128)(2,1)}, bf16[2,32,1536]{2,1,0:T(8,128)(2,1)S(1)}, u32[]{:S(2)}, u32[]{:S(2)}) %collective-permute-start.2) | collective-permute-done | bytes 196640 | tf_op jit(solution)/shard_map/ppermute | solution.py:128
  51.0 6.1 %collective-permute-done.3.refs_4_ = bf16[2,32,1536]{2,1,0:T(8,128)(2,1)S(1)} collective-permute-done((bf16[2,32,1536]{2,1,0:T(8,128)(2,1)}, bf16[2,32,1536]{2,1,0:T(8,128)(2,1)S(1)}, u32[]{:S(2)}, u32[]{:S(2)}) %collective-permute-start.3) | collective-permute-done | bytes 196640 | tf_op jit(solution)/shard_map/ppermute | solution.py:128
  57.1 3.4 %collective-permute-done.4.refs_5_ = bf16[2,32,1536]{2,1,0:T(8,128)(2,1)S(1)} collective-permute-done((bf16[2,32,1536]{2,1,0:T(8,128)(2,1)}, bf16[2,32,1536]{2,1,0:T(8,128)(2,1)S(1)}, u32[]{:S(2)}, u32[]{:S(2)}) %collective-permute-start.4) | collective-permute-done | bytes 196640 | tf_op jit(solution)/shard_map/ppermute | solution.py:128
  62.7 13.0 %all-to-all-done.2.refs_3_ = bf16[16,2,256,128]{3,2,1,0:T(8,128)(2,1)} async-done(((bf16[16,2,256,128]{3,2,1,0:T(8,128)(2,1)}), bf16[16,2,256,128]{3,2,1,0:T(8,128)(2,1)}, u32[]{:S(2)}, u32[]{:S(2)}) %all-to-all-start.2) | async-done | bytes 2097184 | tf_op jit(solution)/shard_map/all_to_all | solution.py:466
  75.7 5.8 %all-to-all-start.1 = ((bf16[16,2,256,128]{3,2,1,0:T(8,128)(2,1)}), bf16[16,2,256,128]{3,2,1,0:T(8,128)(2,1)}, u32[]{:S(2)}, u32[]{:S(2)}) async-start(bf16[16,2,256,128]{3,2,1,0:T(8,128)(2,1)} %copy-done.4), calls=%async_computation.1 | async-start | bytes 4194304 | tf_op jit(solution)/shard_map/all_to_all | solution.py:466
  81.8 1.0 fusion
  83.8 20.1 %attend_first.1.refs_6_ = f32[2,2,144,1536]{3,2,1,0:T(8,128)S(1)} custom-call(s32[2,8]{1,0:T(2,128)S(1)} %and_select_fusion.2.refs_0_, s32[2,2]{1,0:T(2,128)S(1)} %copy-done.9, bf16[2,2,256,1536]{3,2,1,0:T(8,128)(2,1)S(1)} %assemble.1.refs_2_, bf16[16,2,256,128]{3,2,1,0:T(8,128)(2,1)} %all-to-all-done.2.refs_3_, f32[8,128]{1,0:T(8,128)S(1)} %get-tuple-element.53.refs_4_, ...), custom_call_target="tpu_custom_call" | custom-call | flops 8000000000 | bytes 12000000 | tf_op jit(solution)/shard_map/attend_first/pallas_call | solution.py:400
  103.9 1.8 %copy-done.10 = f32[2,2,144,1536]{3,2,1,0:T(8,128)} copy-done((f32[2,2,144,1536]{3,2,1,0:T(8,128)}, f32[2,2,144,1536]{3,2,1,0:T(8,128)S(1)}, u32[]{:S(2)}) %copy-start.10) | copy-done | bytes 3538968
  105.7 3.7 %all-to-all-done.1.refs_3_ = bf16[16,2,256,128]{3,2,1,0:T(8,128)(2,1)} async-done(((bf16[16,2,256,128]{3,2,1,0:T(8,128)(2,1)}), bf16[16,2,256,128]{3,2,1,0:T(8,128)(2,1)}, u32[]{:S(2)}, u32[]{:S(2)}) %all-to-all-start.1) | async-done | bytes 2097184 | tf_op jit(solution)/shard_map/all_to_all | solution.py:466
  109.4 0.9 copy-done.6
  110.4 31.0 %attend_last.1 = (bf16[2,32,1536]{2,1,0:T(8,128)(2,1)S(1)}, bf16[2,32,1536]{2,1,0:T(8,128)(2,1)S(1)}, bf16[2,32,1536]{2,1,0:T(8,128)(2,1)S(1)}, bf16[2,32,1536]{...) custom-call(s32[2,8]{1,0:T(2,128)S(1)} %and_select_fusion.2.refs_0_,, ...), custom_call_target="tpu_custom_call" | custom-call | flops 8000000000 | bytes 12000000 | tf_op jit(solution)/shard_map/attend_last/pallas_call | solution.py:400
  142.1 3.2 %collective-permute-start.10 = (bf16[2,32,1536]{2,1,0:T(8,128)(2,1)S(1)}, bf16[2,32,1536]{2,1,0:T(8,128)(2,1)S(1)}, u32[]{:S(2)}, u32[]{:S(2)}) collective-permute-start(bf16[2,32,1536]{2,1,0:T(8,128)(2,1)S(1)} %get-tuple-element.41), channel_id=1, source_target_pairs={{0,4},{1,5},{2,6},{3,7},{4,0},{5,1},{6,2},{7,3},{8,12},{9,13},{10,... | collective-permute-start | bytes 589832 | tf_op jit(solution)/shard_map/ppermute | solution.py:128
  145.3 1.1 collective-permute-start.12
  146.3 2.5 %collective-permute-start.13 = (bf16[2,32,1536]{2,1,0:T(8,128)(2,1)S(1)}, bf16[2,32,1536]{2,1,0:T(8,128)(2,1)S(1)}, u32[]{:S(2)}, u32[]{:S(2)}) collective-permute-start(bf16[2,32,1536]{2,1,0:T(8,128)(2,1)S(1)} %get-tuple-element.44), channel_id=1, source_target_pairs={{0,7},{1,6},{2,1},{3,0},{4,3},{5,2},{6,5},{7,4},{8,15},{9,14},{10,... | collective-permute-start | bytes 589832 | tf_op jit(solution)/shard_map/ppermute | solution.py:128
  148.8 1.5 collective-permute-done.10.refs_4_
  151.2 2.8 %collective-permute-done.11.refs_5_ = bf16[2,32,1536]{2,1,0:T(8,128)(2,1)S(1)} collective-permute-done((bf16[2,32,1536]{2,1,0:T(8,128)(2,1)S(1)}, bf16[2,32,1536]{2,1,0:T(8,128)(2,1)S(1)}, u32[]{:S(2)}, u32[]{:S(2)}) %collective-permute-start.11) | collective-permute-done | bytes 196640 | tf_op jit(solution)/shard_map/ppermute | solution.py:128
  154.8 4.8 %collective-permute-done.12.refs_6_ = bf16[2,32,1536]{2,1,0:T(8,128)(2,1)S(1)} collective-permute-done((bf16[2,32,1536]{2,1,0:T(8,128)(2,1)S(1)}, bf16[2,32,1536]{2,1,0:T(8,128)(2,1)S(1)}, u32[]{:S(2)}, u32[]{:S(2)}) %collective-permute-start.12) | collective-permute-done | bytes 196640 | tf_op jit(solution)/shard_map/ppermute | solution.py:128
  159.6 1.5 collective-permute-done.13.refs_7_
  162.5 2.7 %join_columns.1 = bf16[2,32,12288]{2,1,0:T(8,128)(2,1)} custom-call(bf16[2,32,1536]{2,1,0:T(8,128)(2,1)} %copy-done.8, bf16[2,32,1536]{2,1,0:T(8,128)(2,1)} %copy-done.15, bf16[2,32,1536]{2,1,0:T(8,128)(2,1)} %copy-done.16, bf16[2,32,1536]{2,1,0:T(8,128)(2,1)} %copy-done.17, bf16[2,32,1536]{2,1,0:T(8,128)(2,1)} %copy-done.11, ...), custom_call_target="tpu_custom_call" | custom-call | tf_op jit(solution)/shard_map/join_columns/pallas_call | solution.py:112
  (65 shorter events, 11.0 us)
Async XLA Ops:
  6.5 2.8 %copy-start = (s32[256]{0:T(256)S(1)}, s32[256]{0:T(256)}, u32[]{:S(2)}) copy-start(s32[256]{0:T(256)} %param.15) | copy-start | bytes 3076
  6.5 17.7 %copy-start.2 = (bf16[16,1,512,128]{3,2,1,0:T(8,128)(2,1)S(1)}, bf16[16,1,512,128]{3,2,1,0:T(8,128)(2,1)}, u32[]{:S(2)}) copy-start(bf16[16,1,512,128]{3,2,1,0:T(8,128)(2,1)} %keys_ref.1) | copy-start | bytes 6291460
  6.5 102.9 %all-gather.2.cloned.1.call-start = ((), (), s32[]{:S(2)}) async-start(), calls=%async_computation.3 | async-start | bytes 6684672 | tf_op jit(solution)/shard_map/all_gather | solution.py:453
  24.2 1.6 copy-start.3
  26.7 1.3 copy-start.4
  28.0 1.3 copy-start.5
  29.3 46.4 %all-to-all-start.2 = ((bf16[16,2,256,128]{3,2,1,0:T(8,128)(2,1)}), bf16[16,2,256,128]{3,2,1,0:T(8,128)(2,1)}, u32[]{:S(2)}, u32[]{:S(2)}) async-start(bf16[16,2,256,128]{3,2,1,0:T(8,128)(2,1)} %copy-done.5), calls=%async_computation.2 | async-start | bytes 4194304 | tf_op jit(solution)/shard_map/all_to_all | solution.py:466
  38.3 6.1 %collective-permute-start = (bf16[2,32,1536]{2,1,0:T(8,128)(2,1)}, bf16[2,32,1536]{2,1,0:T(8,128)(2,1)S(1)}, u32[]{:S(2)}, u32[]{:S(2)}) collective-permute-start(bf16[2,32,1536]{2,1,0:T(8,128)(2,1)} %get-tuple-element.27), channel_id=1, source_target_pairs={{0,1},{1,0},{2,3},{3,2},{4,5},{5,4},{6,7},{7,6},{8,9},{9,8},{10,11... | collective-permute-start | bytes 589832 | tf_op jit(solution)/shard_map/ppermute | solution.py:128
  38.3 9.1 %collective-permute-start.1 = (bf16[2,32,1536]{2,1,0:T(8,128)(2,1)}, bf16[2,32,1536]{2,1,0:T(8,128)(2,1)S(1)}, u32[]{:S(2)}, u32[]{:S(2)}) collective-permute-start(bf16[2,32,1536]{2,1,0:T(8,128)(2,1)} %get-tuple-element.28), channel_id=1, source_target_pairs={{0,2},{1,3},{2,4},{3,5},{4,6},{5,7},{6,0},{7,1},{8,10},{9,11},{10,... | collective-permute-start | bytes 589832 | tf_op jit(solution)/shard_map/ppermute | solution.py:128
  39.9 11.1 %collective-permute-start.2 = (bf16[2,32,1536]{2,1,0:T(8,128)(2,1)}, bf16[2,32,1536]{2,1,0:T(8,128)(2,1)S(1)}, u32[]{:S(2)}, u32[]{:S(2)}) collective-permute-start(bf16[2,32,1536]{2,1,0:T(8,128)(2,1)} %get-tuple-element.29), channel_id=1, source_target_pairs={{0,3},{1,2},{2,5},{3,4},{4,7},{5,6},{6,1},{7,0},{8,11},{9,10},{10,... | collective-permute-start | bytes 589832 | tf_op jit(solution)/shard_map/ppermute | solution.py:128
  41.3 15.8 %collective-permute-start.3 = (bf16[2,32,1536]{2,1,0:T(8,128)(2,1)}, bf16[2,32,1536]{2,1,0:T(8,128)(2,1)S(1)}, u32[]{:S(2)}, u32[]{:S(2)}) collective-permute-start(bf16[2,32,1536]{2,1,0:T(8,128)(2,1)} %get-tuple-element.30), channel_id=1, source_target_pairs={{0,4},{1,5},{2,6},{3,7},{4,0},{5,1},{6,2},{7,3},{8,12},{9,13},{10,... | collective-permute-start | bytes 589832 | tf_op jit(solution)/shard_map/ppermute | solution.py:128
  42.9 17.6 %collective-permute-start.4 = (bf16[2,32,1536]{2,1,0:T(8,128)(2,1)}, bf16[2,32,1536]{2,1,0:T(8,128)(2,1)S(1)}, u32[]{:S(2)}, u32[]{:S(2)}) collective-permute-start(bf16[2,32,1536]{2,1,0:T(8,128)(2,1)} %get-tuple-element.31), channel_id=1, source_target_pairs={{0,5},{1,4},{2,7},{3,6},{4,1},{5,0},{6,3},{7,2},{8,13},{9,12},{10,... | collective-permute-start | bytes 589832 | tf_op jit(solution)/shard_map/ppermute | solution.py:128
  44.4 16.1 %collective-permute-start.5 = (bf16[2,32,1536]{2,1,0:T(8,128)(2,1)}, bf16[2,32,1536]{2,1,0:T(8,128)(2,1)S(1)}, u32[]{:S(2)}, u32[]{:S(2)}) collective-permute-start(bf16[2,32,1536]{2,1,0:T(8,128)(2,1)} %get-tuple-element.32), channel_id=1, source_target_pairs={{0,6},{1,7},{2,0},{3,1},{4,2},{5,3},{6,4},{7,5},{8,14},{9,15},{10,... | collective-permute-start | bytes 589832 | tf_op jit(solution)/shard_map/ppermute | solution.py:128
  47.4 13.7 %collective-permute-start.6 = (bf16[2,32,1536]{2,1,0:T(8,128)(2,1)}, bf16[2,32,1536]{2,1,0:T(8,128)(2,1)S(1)}, u32[]{:S(2)}, u32[]{:S(2)}) collective-permute-start(bf16[2,32,1536]{2,1,0:T(8,128)(2,1)} %get-tuple-element.33), channel_id=1, source_target_pairs={{0,7},{1,6},{2,1},{3,0},{4,3},{5,2},{6,5},{7,4},{8,15},{9,14},{10,... | collective-permute-start | bytes 589832 | tf_op jit(solution)/shard_map/ppermute | solution.py:128
  61.1 0.9 copy-start.7
  62.7 21.1 %copy-start.1 = (bf16[2,2,256,1536]{3,2,1,0:T(8,128)(2,1)}, bf16[2,2,256,1536]{3,2,1,0:T(8,128)(2,1)S(1)}, u32[]{:S(2)}) copy-start(bf16[2,2,256,1536]{3,2,1,0:T(8,128)(2,1)S(1)} %assemble.1.refs_2_) | copy-start | bytes 9437188
  62.7 19.0 %copy-start.9 = (s32[2,2]{1,0:T(2,128)S(1)}, s32[2,2]{1,0:T(2,128)}, u32[]{:S(2)}) copy-start(s32[2,2]{1,0:T(2,128)} %refs_1_.3) | copy-start | bytes 52
  75.7 33.8 %all-to-all-start.1 = ((bf16[16,2,256,128]{3,2,1,0:T(8,128)(2,1)}), bf16[16,2,256,128]{3,2,1,0:T(8,128)(2,1)}, u32[]{:S(2)}, u32[]{:S(2)}) async-start(bf16[16,2,256,128]{3,2,1,0:T(8,128)(2,1)} %copy-done.4), calls=%async_computation.1 | async-start | bytes 4194304 | tf_op jit(solution)/shard_map/all_to_all | solution.py:466
  103.9 1.8 %copy-start.10 = (f32[2,2,144,1536]{3,2,1,0:T(8,128)}, f32[2,2,144,1536]{3,2,1,0:T(8,128)S(1)}, u32[]{:S(2)}) copy-start(f32[2,2,144,1536]{3,2,1,0:T(8,128)S(1)} %attend_first.1.refs_6_) | copy-start | bytes 10616836
  109.4 1.0 copy-start.6
  142.1 8.3 %collective-permute-start.10 = (bf16[2,32,1536]{2,1,0:T(8,128)(2,1)S(1)}, bf16[2,32,1536]{2,1,0:T(8,128)(2,1)S(1)}, u32[]{:S(2)}, u32[]{:S(2)}) collective-permute-start(bf16[2,32,1536]{2,1,0:T(8,128)(2,1)S(1)} %get-tuple-element.41), channel_id=1, source_target_pairs={{0,4},{1,5},{2,6},{3,7},{4,0},{5,1},{6,2},{7,3},{8,12},{9,13},{10,... | collective-permute-start | bytes 589832 | tf_op jit(solution)/shard_map/ppermute | solution.py:128
  145.2 8.8 %collective-permute-start.11 = (bf16[2,32,1536]{2,1,0:T(8,128)(2,1)S(1)}, bf16[2,32,1536]{2,1,0:T(8,128)(2,1)S(1)}, u32[]{:S(2)}, u32[]{:S(2)}) collective-permute-start(bf16[2,32,1536]{2,1,0:T(8,128)(2,1)S(1)} %get-tuple-element.42), channel_id=1, source_target_pairs={{0,5},{1,4},{2,7},{3,6},{4,1},{5,0},{6,3},{7,2},{8,13},{9,12},{10,... | collective-permute-start | bytes 589832 | tf_op jit(solution)/shard_map/ppermute | solution.py:128
  145.3 14.3 %collective-permute-start.12 = (bf16[2,32,1536]{2,1,0:T(8,128)(2,1)S(1)}, bf16[2,32,1536]{2,1,0:T(8,128)(2,1)S(1)}, u32[]{:S(2)}, u32[]{:S(2)}) collective-permute-start(bf16[2,32,1536]{2,1,0:T(8,128)(2,1)S(1)} %get-tuple-element.43), channel_id=1, source_target_pairs={{0,6},{1,7},{2,0},{3,1},{4,2},{5,3},{6,4},{7,5},{8,14},{9,15},{10,... | collective-permute-start | bytes 589832 | tf_op jit(solution)/shard_map/ppermute | solution.py:128
  146.3 14.8 %collective-permute-start.13 = (bf16[2,32,1536]{2,1,0:T(8,128)(2,1)S(1)}, bf16[2,32,1536]{2,1,0:T(8,128)(2,1)S(1)}, u32[]{:S(2)}, u32[]{:S(2)}) collective-permute-start(bf16[2,32,1536]{2,1,0:T(8,128)(2,1)S(1)} %get-tuple-element.44), channel_id=1, source_target_pairs={{0,7},{1,6},{2,1},{3,0},{4,3},{5,2},{6,5},{7,4},{8,15},{9,14},{10,... | collective-permute-start | bytes 589832 | tf_op jit(solution)/shard_map/ppermute | solution.py:128
  148.8 12.3 %collective-permute-start.7 = (bf16[2,32,1536]{2,1,0:T(8,128)(2,1)S(1)}, bf16[2,32,1536]{2,1,0:T(8,128)(2,1)S(1)}, u32[]{:S(2)}, u32[]{:S(2)}) collective-permute-start(bf16[2,32,1536]{2,1,0:T(8,128)(2,1)S(1)} %get-tuple-element.38), channel_id=1, source_target_pairs={{0,1},{1,0},{2,3},{3,2},{4,5},{5,4},{6,7},{7,6},{8,9},{9,8},{10,11... | collective-permute-start | bytes 589832 | tf_op jit(solution)/shard_map/ppermute | solution.py:128
  150.3 11.6 %copy-start.11 = (bf16[2,32,1536]{2,1,0:T(8,128)(2,1)}, bf16[2,32,1536]{2,1,0:T(8,128)(2,1)S(1)}, u32[]{:S(2)}) copy-start(bf16[2,32,1536]{2,1,0:T(8,128)(2,1)S(1)} %collective-permute-done.10.refs_4_) | copy-start | bytes 589828
  150.3 10.8 %collective-permute-start.8 = (bf16[2,32,1536]{2,1,0:T(8,128)(2,1)S(1)}, bf16[2,32,1536]{2,1,0:T(8,128)(2,1)S(1)}, u32[]{:S(2)}, u32[]{:S(2)}) collective-permute-start(bf16[2,32,1536]{2,1,0:T(8,128)(2,1)S(1)} %get-tuple-element.39), channel_id=1, source_target_pairs={{0,2},{1,3},{2,4},{3,5},{4,6},{5,7},{6,0},{7,1},{8,10},{9,11},{10,... | collective-permute-start | bytes 589832 | tf_op jit(solution)/shard_map/ppermute | solution.py:128
  154.1 7.8 %copy-start.12 = (bf16[2,32,1536]{2,1,0:T(8,128)(2,1)}, bf16[2,32,1536]{2,1,0:T(8,128)(2,1)S(1)}, u32[]{:S(2)}) copy-start(bf16[2,32,1536]{2,1,0:T(8,128)(2,1)S(1)} %collective-permute-done.11.refs_5_) | copy-start | bytes 589828
  154.1 7.8 %collective-permute-start.9 = (bf16[2,32,1536]{2,1,0:T(8,128)(2,1)S(1)}, bf16[2,32,1536]{2,1,0:T(8,128)(2,1)S(1)}, u32[]{:S(2)}, u32[]{:S(2)}) collective-permute-start(bf16[2,32,1536]{2,1,0:T(8,128)(2,1)S(1)} %get-tuple-element.40), channel_id=1, source_target_pairs={{0,3},{1,2},{2,5},{3,4},{4,7},{5,6},{6,1},{7,0},{8,11},{9,10},{10,... | collective-permute-start | bytes 589832 | tf_op jit(solution)/shard_map/ppermute | solution.py:128
  159.6 2.3 %copy-start.13 = (bf16[2,32,1536]{2,1,0:T(8,128)(2,1)}, bf16[2,32,1536]{2,1,0:T(8,128)(2,1)S(1)}, u32[]{:S(2)}) copy-start(bf16[2,32,1536]{2,1,0:T(8,128)(2,1)S(1)} %collective-permute-done.12.refs_6_) | copy-start | bytes 589828
  161.1 0.8 copy-start.15
  161.1 0.8 copy-start.16
  (3 other events, 2.1 us)
Sparse Core Ops, SparseCore 0:
  9.5 96.7 all-gather.1

commit v5 on v4

--- a/solution.py
+++ b/solution.py
@@ -51,7 +51,7 @@
 def split_columns(x, pieces):
     lead, rows, width = x.shape
     out = jax.ShapeDtypeStruct((lead, rows, width // pieces), x.dtype)
-    return pl.pallas_call(split_kernel, out_shape=[out] * pieces, name="split_columns")(x)
+    return pl.pallas_call(split_kernel, out_shape=[out] * pieces, compiler_params=pltpu.CompilerParams(vmem_limit_bytes=8 * 2**20), name="split_columns")(x)
 
 
 def assemble_kernel(*refs):
@@ -115,6 +115,7 @@
         out_specs=pl.BlockSpec(memory_space=pltpu.HBM),
         out_shape=jax.ShapeDtypeStruct((lead, rows, len(pieces) * part), pieces[0].dtype),
         scratch_shapes=[pltpu.SemaphoreType.DMA((len(pieces),))],
+        compiler_params=pltpu.CompilerParams(vmem_limit_bytes=8 * 2**20),
         name="join_columns",
     )(*pieces)
 
@@ -129,33 +130,28 @@
     return received
 
 
-def pick_kernel(rows_ref, keys_ref, values_ref, *o_refs):
+def pick_kernel(start, rows_ref, keys_ref, values_ref, o_ref):
+    at = slice(start, start + o_ref.shape[2])
+
     def step(d, carry):
         row = rows_ref[d]
-        start = 0
-        for o_ref in o_refs:
-            at = slice(start, start + o_ref.shape[2])
-            o_ref[d, 0] = keys_ref[row, 0, at]
-            o_ref[d, 1] = values_ref[row, 0, at]
-            start = at.stop
+        o_ref[d, 0] = keys_ref[row, 0, at]
+        o_ref[d, 1] = values_ref[row, 0, at]
         return carry
 
-    lax.fori_loop(0, o_refs[0].shape[0], step, 0)
-
-
-def pick_spans(rows, keys, values, pieces):
+    lax.fori_loop(0, o_ref.shape[0], step, 0)
+
+
+def pick_spans(rows, keys, values, piece, pieces):
     count = rows.shape[0]
     span_len, head_dim = keys.shape[2:]
-    out = jax.ShapeDtypeStruct((count, 2, span_len // pieces, head_dim), keys.dtype)
+    part = span_len // pieces
+    vmem = pl.BlockSpec(memory_space=pltpu.VMEM)
     return pl.pallas_call(
-        pick_kernel,
-        in_specs=[
-            pl.BlockSpec(memory_space=pltpu.SMEM),
-            pl.BlockSpec(memory_space=pltpu.VMEM),
-            pl.BlockSpec(memory_space=pltpu.VMEM),
-        ],
-        out_specs=[pl.BlockSpec(memory_space=pltpu.VMEM)] * pieces,
-        out_shape=[out] * pieces,
+        functools.partial(pick_kernel, piece * part),
+        in_specs=[pl.BlockSpec(memory_space=pltpu.SMEM), vmem, vmem],
+        out_specs=vmem,
+        out_shape=jax.ShapeDtypeStruct((count, 2, part, head_dim), keys.dtype),
         compiler_params=pltpu.CompilerParams(vmem_limit_bytes=20 * 2**20),
         name="pick_spans",
     )(rows, keys, values)
@@ -454,16 +450,24 @@
         jnp.concatenate([key_weight, value_weight], axis=1), "store", axis=0, tiled=True
     )
     pieces = 2
-    picked = pick_spans(incoming.reshape(-1), span_keys, span_values, pieces)
+    rows = incoming.reshape(-1)
     split = split_columns(tile_queries, head_count)
     received = head_exchange(split)
     queries = assemble(received, recompute, head_dim)
 
     got = []
-    for part in picked:
+    for piece in range(pieces):
         if got:
-            part, queries = lax.optimization_barrier((part, queries))
-        got.append(lax.all_to_all(part, "store", split_axis=0, concat_axis=0, tiled=True))
+            rows, queries = lax.optimization_barrier((rows, queries))
+        got.append(
+            lax.all_to_all(
+                pick_spans(rows, span_keys, span_values, piece, pieces),
+                "store",
+                split_axis=0,
+                concat_axis=0,
+                tiled=True,
+            )
+        )
 
     offsets = jnp.arange(tile_len, dtype=jnp.int32)
     positions = (tile_ids[:, :, None] * tile_len + offsets).reshape(-1)

time: 174 us -> 168 us (0.966)
  Pallas kernels: 58 us -> 47.2 us
  waiting for transfers between devices: 42.2 us -> 44.7 us
    pallas_call x2, Pallas kernels: 51.1 us -> 43.8 us  [attend(): pl.pallas_call(functools.partial(attend_kernel, exp_scale, tile_len, piec...]
    all_to_all x2, waiting for transfers between devices: 16.7 us -> 19.6 us  [body(): lax.all_to_all(pick_spans(rows, span_keys, span_values, piece, pieces), '...]
    pallas_call x2 -> x3, Pallas kernels: 3.56 us -> 1.6 us  [the longest x2 1.5 us: pick_spans(): pl.pallas_call(functools.partial(pick_kernel, piece * part), in_specs=[pl...]
    unnamed x36 -> x24, local copies, waits for them, and re-layouts: 9.23 us -> 10.1 us
  transfers between devices with their start and end apart: 17 -> 17, of which waited for: 12 -> 12; matrix products, arithmetic and copies ran while one was open for 3% -> 3% of each run, Pallas kernels for 14% -> 11%
where the time goes in v5:
time: 168 us; the launch traced here: 166 us
  Pallas kernels  47.2 us (28%)
  waiting for transfers between devices  44.7 us (27%)
  starting transfers between devices  30.1 us (18%)
  blocking collectives  13.6 us (8%)
  between operations  13.6 us (8%)
  local copies, waits for them, and re-layouts  11 us (7%)
  other arithmetic  5.33 us (3%)
    pallas_call x2, Pallas kernels, attend(): pl.pallas_call(functools.partial(attend_kernel, exp_scale, tile_len, piec...  43.8 us
    ppermute x14, waiting for transfers between devices, head_exchange(): received.append(lax.ppermute(pieces[step], 'head', pairs))  25.1 us
    all_to_all x2, waiting for transfers between devices, body(): lax.all_to_all(pick_spans(rows, span_keys, span_values, piece, pieces), '...  19.6 us
    ppermute x14, starting transfers between devices, head_exchange(): received.append(lax.ppermute(pieces[step], 'head', pairs))  17.6 us
    all_to_all x1, blocking collectives, body(): lax.all_to_all(wanted.reshape(store_count, 1), 'store', split_axis=0, con...  13.6 us
    all_to_all x2, starting transfers between devices, body(): lax.all_to_all(pick_spans(rows, span_keys, span_values, piece, pieces), '...  12.4 us
    unnamed x24, local copies, waits for them, and re-layouts  10.1 us
  transfers between devices with their start and end apart: 17, of which 12 were waited for; matrix products, arithmetic and copies ran while one was open for 3% of the time, Pallas kernels for 11%

profile of v5, /device:TPU:6, one launch (start us, length us, event | category | flops | bytes accessed | tf_op | source)
XLA Modules:
  0.0 165.6 jit_solution(10350385539215853750)
XLA Ops:
  6.5 2.0 %pad_maximum_fusion = bf16[768,256]{1,0:T(8,128)(2,1)} fusion(bf16[768,128]{1,0:T(8,128)(2,1)} %param.12, bf16[768,128]{1,0:T(8,128)(2,1)} %param.11), kind=kLoop, calls=%fused_computation.1 | loop fusion | flops 786432 | bytes 786432 | tf_op jit(solution)/shard_map/concatenate | solution.py:450
  10.2 13.6 %all_to_all.19 = s32[16,1,1]{2,1,0:T(1,128)S(1)} all-to-all(s32[16,1,1]{2,1,0:T(1,128)S(1)} %copy.12), channel_id=1, replica_groups=mesh['store'=16,'head'=8] {'store'}, dimensions={0} | all-to-all | bytes 128 | tf_op jit(solution)/shard_map/all_to_all | solution.py:446
  24.2 1.6 copy-done.2
  26.6 1.3 copy-done.4
  27.9 6.3 %all-to-all-start.2 = ((bf16[16,2,256,128]{3,2,1,0:T(8,128)(2,1)}), bf16[16,2,256,128]{3,2,1,0:T(8,128)(2,1)}, u32[]{:S(2)}, u32[]{:S(2)}) async-start(bf16[16,2,256,128]{3,2,1,0:T(8,128)(2,1)} %copy-done.4), calls=%async_computation.2 | async-start | bytes 4194304 | tf_op jit(solution)/shard_map/all_to_all | solution.py:463
  34.2 1.4 copy-done.8
  35.8 1.6 collective-permute-start.1
  37.4 1.3 collective-permute-start.2
  38.8 1.6 collective-permute-start.3
  40.4 1.6 collective-permute-start.4
  42.0 1.7 %collective-permute-start.5 = (bf16[2,32,1536]{2,1,0:T(8,128)(2,1)S(1)}, bf16[2,32,1536]{2,1,0:T(8,128)(2,1)S(1)}, u32[]{:S(2)}, u32[]{:S(2)}) collective-permute-start(bf16[2,32,1536]{2,1,0:T(8,128)(2,1)S(1)} %get-tuple-element.29), channel_id=1, source_target_pairs={{0,6},{1,7},{2,0},{3,1},{4,2},{5,3},{6,4},{7,5},{8,14},{9,15},{10,... | collective-permute-start | bytes 589832 | tf_op jit(solution)/shard_map/ppermute | solution.py:129
  43.7 1.1 collective-permute-done.1.refs_2_
  45.5 2.7 %collective-permute-done.2.refs_3_ = bf16[2,32,1536]{2,1,0:T(8,128)(2,1)S(1)} collective-permute-done((bf16[2,32,1536]{2,1,0:T(8,128)(2,1)S(1)}, bf16[2,32,1536]{2,1,0:T(8,128)(2,1)S(1)}, u32[]{:S(2)}, u32[]{:S(2)}) %collective-permute-start.2) | collective-permute-done | bytes 196640 | tf_op jit(solution)/shard_map/ppermute | solution.py:129
  48.2 6.3 %collective-permute-done.3.refs_4_ = bf16[2,32,1536]{2,1,0:T(8,128)(2,1)S(1)} collective-permute-done((bf16[2,32,1536]{2,1,0:T(8,128)(2,1)S(1)}, bf16[2,32,1536]{2,1,0:T(8,128)(2,1)S(1)}, u32[]{:S(2)}, u32[]{:S(2)}) %collective-permute-start.3) | collective-permute-done | bytes 196640 | tf_op jit(solution)/shard_map/ppermute | solution.py:129
  54.5 3.3 %collective-permute-done.4.refs_5_ = bf16[2,32,1536]{2,1,0:T(8,128)(2,1)S(1)} collective-permute-done((bf16[2,32,1536]{2,1,0:T(8,128)(2,1)S(1)}, bf16[2,32,1536]{2,1,0:T(8,128)(2,1)S(1)}, u32[]{:S(2)}, u32[]{:S(2)}) %collective-permute-start.4) | collective-permute-done | bytes 196640 | tf_op jit(solution)/shard_map/ppermute | solution.py:129
  59.2 1.7 %copy-done.6 = bf16[2,2,256,1536]{3,2,1,0:T(8,128)(2,1)} copy-done((bf16[2,2,256,1536]{3,2,1,0:T(8,128)(2,1)}, bf16[2,2,256,1536]{3,2,1,0:T(8,128)(2,1)S(1)}, u32[]{:S(2)}) %copy-start.6) | copy-done | bytes 3145752
  61.7 1.3 copy-done.5
  63.0 5.9 %all-to-all-done.2.refs_3_ = bf16[16,2,256,128]{3,2,1,0:T(8,128)(2,1)} async-done(((bf16[16,2,256,128]{3,2,1,0:T(8,128)(2,1)}), bf16[16,2,256,128]{3,2,1,0:T(8,128)(2,1)}, u32[]{:S(2)}, u32[]{:S(2)}) %all-to-all-start.2) | async-done | bytes 2097184 | tf_op jit(solution)/shard_map/all_to_all | solution.py:463
  68.9 6.1 %all-to-all-start.1 = ((bf16[16,2,256,128]{3,2,1,0:T(8,128)(2,1)}), bf16[16,2,256,128]{3,2,1,0:T(8,128)(2,1)}, u32[]{:S(2)}, u32[]{:S(2)}) async-start(bf16[16,2,256,128]{3,2,1,0:T(8,128)(2,1)} %copy-done.5), calls=%async_computation.1 | async-start | bytes 4194304 | tf_op jit(solution)/shard_map/all_to_all | solution.py:463
  77.2 15.6 %attend_first.1.refs_6_ = f32[2,2,144,1536]{3,2,1,0:T(8,128)S(1)} custom-call(s32[2,8]{1,0:T(2,128)S(1)} %and_select_fusion.2.refs_0_, s32[2,2]{1,0:T(2,128)S(1)} %copy-done.10, bf16[2,2,256,1536]{3,2,1,0:T(8,128)(2,1)S(1)} %copy-done.7, bf16[16,2,256,128]{3,2,1,0:T(8,128)(2,1)} %all-to-all-done.2.refs_3_, f32[8,128]{1,0:T(8,128)S(1)} %get-tuple-element.49.refs_4_, ...), custom_call_target="tpu_custom_call" | custom-call | flops 8000000000 | bytes 12000000 | tf_op jit(solution)/shard_map/attend_first/pallas_call | solution.py:396
  92.9 1.8 %copy-done.11 = f32[2,2,144,1536]{3,2,1,0:T(8,128)} copy-done((f32[2,2,144,1536]{3,2,1,0:T(8,128)}, f32[2,2,144,1536]{3,2,1,0:T(8,128)S(1)}, u32[]{:S(2)}) %copy-start.11) | copy-done | bytes 3538968
  94.7 13.8 %all-to-all-done.1.refs_3_ = bf16[16,2,256,128]{3,2,1,0:T(8,128)(2,1)} async-done(((bf16[16,2,256,128]{3,2,1,0:T(8,128)(2,1)}), bf16[16,2,256,128]{3,2,1,0:T(8,128)(2,1)}, u32[]{:S(2)}, u32[]{:S(2)}) %all-to-all-start.1) | async-done | bytes 2097184 | tf_op jit(solution)/shard_map/all_to_all | solution.py:463
  109.4 28.2 %attend_last.1 = (bf16[2,32,1536]{2,1,0:T(8,128)(2,1)S(1)}, bf16[2,32,1536]{2,1,0:T(8,128)(2,1)S(1)}, bf16[2,32,1536]{2,1,0:T(8,128)(2,1)S(1)}, bf16[2,32,1536]{...) custom-call(s32[2,8]{1,0:T(2,128)S(1)} %and_select_fusion.2.refs_0_,, ...), custom_call_target="tpu_custom_call" | custom-call | flops 8000000000 | bytes 12000000 | tf_op jit(solution)/shard_map/attend_last/pallas_call | solution.py:396
  137.6 3.1 %collective-permute-start.10 = (bf16[2,32,1536]{2,1,0:T(8,128)(2,1)S(1)}, bf16[2,32,1536]{2,1,0:T(8,128)(2,1)S(1)}, u32[]{:S(2)}, u32[]{:S(2)}) collective-permute-start(bf16[2,32,1536]{2,1,0:T(8,128)(2,1)S(1)} %get-tuple-element.37), channel_id=1, source_target_pairs={{0,4},{1,5},{2,6},{3,7},{4,0},{5,1},{6,2},{7,3},{8,12},{9,13},{10,... | collective-permute-start | bytes 589832 | tf_op jit(solution)/shard_map/ppermute | solution.py:129
  140.7 1.4 collective-permute-start.12
  142.1 2.2 %collective-permute-start.13 = (bf16[2,32,1536]{2,1,0:T(8,128)(2,1)S(1)}, bf16[2,32,1536]{2,1,0:T(8,128)(2,1)S(1)}, u32[]{:S(2)}, u32[]{:S(2)}) collective-permute-start(bf16[2,32,1536]{2,1,0:T(8,128)(2,1)S(1)} %get-tuple-element.40), channel_id=1, source_target_pairs={{0,7},{1,6},{2,1},{3,0},{4,3},{5,2},{6,5},{7,4},{8,15},{9,14},{10,... | collective-permute-start | bytes 589832 | tf_op jit(solution)/shard_map/ppermute | solution.py:129
  144.2 1.7 %collective-permute-done.10.refs_4_ = bf16[2,32,1536]{2,1,0:T(8,128)(2,1)S(1)} collective-permute-done((bf16[2,32,1536]{2,1,0:T(8,128)(2,1)S(1)}, bf16[2,32,1536]{2,1,0:T(8,128)(2,1)S(1)}, u32[]{:S(2)}, u32[]{:S(2)}) %collective-permute-start.10) | collective-permute-done | bytes 196640 | tf_op jit(solution)/shard_map/ppermute | solution.py:129
  146.0 1.3 collective-permute-start.8
  147.3 2.6 %collective-permute-done.11.refs_5_ = bf16[2,32,1536]{2,1,0:T(8,128)(2,1)S(1)} collective-permute-done((bf16[2,32,1536]{2,1,0:T(8,128)(2,1)S(1)}, bf16[2,32,1536]{2,1,0:T(8,128)(2,1)S(1)}, u32[]{:S(2)}, u32[]{:S(2)}) %collective-permute-start.11) | collective-permute-done | bytes 196640 | tf_op jit(solution)/shard_map/ppermute | solution.py:129
  150.9 3.7 %collective-permute-done.12.refs_6_ = bf16[2,32,1536]{2,1,0:T(8,128)(2,1)S(1)} collective-permute-done((bf16[2,32,1536]{2,1,0:T(8,128)(2,1)S(1)}, bf16[2,32,1536]{2,1,0:T(8,128)(2,1)S(1)}, u32[]{:S(2)}, u32[]{:S(2)}) %collective-permute-start.12) | collective-permute-done | bytes 196640 | tf_op jit(solution)/shard_map/ppermute | solution.py:129
  154.6 1.9 %collective-permute-done.13.refs_7_ = bf16[2,32,1536]{2,1,0:T(8,128)(2,1)S(1)} collective-permute-done((bf16[2,32,1536]{2,1,0:T(8,128)(2,1)S(1)}, bf16[2,32,1536]{2,1,0:T(8,128)(2,1)S(1)}, u32[]{:S(2)}, u32[]{:S(2)}) %collective-permute-start.13) | collective-permute-done | bytes 196640 | tf_op jit(solution)/shard_map/ppermute | solution.py:129
  157.5 1.2 join_columns.1
  (54 shorter events, 11.1 us)
Async XLA Ops:
  6.5 2.8 %copy-start = (s32[256]{0:T(256)S(1)}, s32[256]{0:T(256)}, u32[]{:S(2)}) copy-start(s32[256]{0:T(256)} %param.15) | copy-start | bytes 3076
  6.5 17.7 %copy-start.1 = (bf16[16,1,512,128]{3,2,1,0:T(8,128)(2,1)S(1)}, bf16[16,1,512,128]{3,2,1,0:T(8,128)(2,1)}, u32[]{:S(2)}) copy-start(bf16[16,1,512,128]{3,2,1,0:T(8,128)(2,1)} %keys_ref.3) | copy-start | bytes 6291460
  6.5 101.9 %all-gather.2.cloned.1.call-start = ((), (), s32[]{:S(2)}) async-start(), calls=%async_computation.3 | async-start | bytes 6684672 | tf_op jit(solution)/shard_map/all_gather | solution.py:449
  24.2 1.6 copy-start.2
  26.6 1.3 copy-start.4
  27.9 41.0 %all-to-all-start.2 = ((bf16[16,2,256,128]{3,2,1,0:T(8,128)(2,1)}), bf16[16,2,256,128]{3,2,1,0:T(8,128)(2,1)}, u32[]{:S(2)}, u32[]{:S(2)}) async-start(bf16[16,2,256,128]{3,2,1,0:T(8,128)(2,1)} %copy-done.4), calls=%async_computation.2 | async-start | bytes 4194304 | tf_op jit(solution)/shard_map/all_to_all | solution.py:463
  34.2 1.4 copy-start.8
  35.7 6.3 %collective-permute-start = (bf16[2,32,1536]{2,1,0:T(8,128)(2,1)S(1)}, bf16[2,32,1536]{2,1,0:T(8,128)(2,1)S(1)}, u32[]{:S(2)}, u32[]{:S(2)}) collective-permute-start(bf16[2,32,1536]{2,1,0:T(8,128)(2,1)S(1)} %get-tuple-element.24), channel_id=1, source_target_pairs={{0,1},{1,0},{2,3},{3,2},{4,5},{5,4},{6,7},{7,6},{8,9},{9,8},{10,11... | collective-permute-start | bytes 589832 | tf_op jit(solution)/shard_map/ppermute | solution.py:129
  35.8 9.0 %collective-permute-start.1 = (bf16[2,32,1536]{2,1,0:T(8,128)(2,1)S(1)}, bf16[2,32,1536]{2,1,0:T(8,128)(2,1)S(1)}, u32[]{:S(2)}, u32[]{:S(2)}) collective-permute-start(bf16[2,32,1536]{2,1,0:T(8,128)(2,1)S(1)} %get-tuple-element.25), channel_id=1, source_target_pairs={{0,2},{1,3},{2,4},{3,5},{4,6},{5,7},{6,0},{7,1},{8,10},{9,11},{10,... | collective-permute-start | bytes 589832 | tf_op jit(solution)/shard_map/ppermute | solution.py:129
  37.4 10.7 %collective-permute-start.2 = (bf16[2,32,1536]{2,1,0:T(8,128)(2,1)S(1)}, bf16[2,32,1536]{2,1,0:T(8,128)(2,1)S(1)}, u32[]{:S(2)}, u32[]{:S(2)}) collective-permute-start(bf16[2,32,1536]{2,1,0:T(8,128)(2,1)S(1)} %get-tuple-element.26), channel_id=1, source_target_pairs={{0,3},{1,2},{2,5},{3,4},{4,7},{5,6},{6,1},{7,0},{8,11},{9,10},{10,... | collective-permute-start | bytes 589832 | tf_op jit(solution)/shard_map/ppermute | solution.py:129
  38.8 15.7 %collective-permute-start.3 = (bf16[2,32,1536]{2,1,0:T(8,128)(2,1)S(1)}, bf16[2,32,1536]{2,1,0:T(8,128)(2,1)S(1)}, u32[]{:S(2)}, u32[]{:S(2)}) collective-permute-start(bf16[2,32,1536]{2,1,0:T(8,128)(2,1)S(1)} %get-tuple-element.27), channel_id=1, source_target_pairs={{0,4},{1,5},{2,6},{3,7},{4,0},{5,1},{6,2},{7,3},{8,12},{9,13},{10,... | collective-permute-start | bytes 589832 | tf_op jit(solution)/shard_map/ppermute | solution.py:129
  40.4 17.3 %collective-permute-start.4 = (bf16[2,32,1536]{2,1,0:T(8,128)(2,1)S(1)}, bf16[2,32,1536]{2,1,0:T(8,128)(2,1)S(1)}, u32[]{:S(2)}, u32[]{:S(2)}) collective-permute-start(bf16[2,32,1536]{2,1,0:T(8,128)(2,1)S(1)} %get-tuple-element.28), channel_id=1, source_target_pairs={{0,5},{1,4},{2,7},{3,6},{4,1},{5,0},{6,3},{7,2},{8,13},{9,12},{10,... | collective-permute-start | bytes 589832 | tf_op jit(solution)/shard_map/ppermute | solution.py:129
  42.0 15.7 %collective-permute-start.5 = (bf16[2,32,1536]{2,1,0:T(8,128)(2,1)S(1)}, bf16[2,32,1536]{2,1,0:T(8,128)(2,1)S(1)}, u32[]{:S(2)}, u32[]{:S(2)}) collective-permute-start(bf16[2,32,1536]{2,1,0:T(8,128)(2,1)S(1)} %get-tuple-element.29), channel_id=1, source_target_pairs={{0,6},{1,7},{2,0},{3,1},{4,2},{5,3},{6,4},{7,5},{8,14},{9,15},{10,... | collective-permute-start | bytes 589832 | tf_op jit(solution)/shard_map/ppermute | solution.py:129
  44.8 13.8 %collective-permute-start.6 = (bf16[2,32,1536]{2,1,0:T(8,128)(2,1)S(1)}, bf16[2,32,1536]{2,1,0:T(8,128)(2,1)S(1)}, u32[]{:S(2)}, u32[]{:S(2)}) collective-permute-start(bf16[2,32,1536]{2,1,0:T(8,128)(2,1)S(1)} %get-tuple-element.30), channel_id=1, source_target_pairs={{0,7},{1,6},{2,1},{3,0},{4,3},{5,2},{6,5},{7,4},{8,15},{9,14},{10,... | collective-permute-start | bytes 589832 | tf_op jit(solution)/shard_map/ppermute | solution.py:129
  58.5 2.4 %copy-start.3 = (bf16[16,1,512,128]{3,2,1,0:T(8,128)(2,1)S(1)}, bf16[16,1,512,128]{3,2,1,0:T(8,128)(2,1)}, u32[]{:S(2)}) copy-start(bf16[16,1,512,128]{3,2,1,0:T(8,128)(2,1)} %values_ref.3) | copy-start | bytes 6291460
  59.2 1.7 %copy-start.6 = (bf16[2,2,256,1536]{3,2,1,0:T(8,128)(2,1)}, bf16[2,2,256,1536]{3,2,1,0:T(8,128)(2,1)S(1)}, u32[]{:S(2)}) copy-start(bf16[2,2,256,1536]{3,2,1,0:T(8,128)(2,1)S(1)} %assemble.1.refs_2_) | copy-start | bytes 9437188
  61.7 1.3 copy-start.5
  63.0 12.3 %copy-start.10 = (s32[2,2]{1,0:T(2,128)S(1)}, s32[2,2]{1,0:T(2,128)}, u32[]{:S(2)}) copy-start(s32[2,2]{1,0:T(2,128)} %refs_1_.3) | copy-start | bytes 52
  68.9 8.4 %copy-start.7 = (bf16[2,2,256,1536]{3,2,1,0:T(8,128)(2,1)S(1)}, bf16[2,2,256,1536]{3,2,1,0:T(8,128)(2,1)}, u32[]{:S(2)}) copy-start(bf16[2,2,256,1536]{3,2,1,0:T(8,128)(2,1)} %copy-done.6) | copy-start | bytes 9437188
  68.9 39.6 %all-to-all-start.1 = ((bf16[16,2,256,128]{3,2,1,0:T(8,128)(2,1)}), bf16[16,2,256,128]{3,2,1,0:T(8,128)(2,1)}, u32[]{:S(2)}, u32[]{:S(2)}) async-start(bf16[16,2,256,128]{3,2,1,0:T(8,128)(2,1)} %copy-done.5), calls=%async_computation.1 | async-start | bytes 4194304 | tf_op jit(solution)/shard_map/all_to_all | solution.py:463
  92.9 1.8 %copy-start.11 = (f32[2,2,144,1536]{3,2,1,0:T(8,128)}, f32[2,2,144,1536]{3,2,1,0:T(8,128)S(1)}, u32[]{:S(2)}) copy-start(f32[2,2,144,1536]{3,2,1,0:T(8,128)S(1)} %attend_first.1.refs_6_) | copy-start | bytes 10616836
  108.5 1.0 copy-start.9
  137.6 8.4 %collective-permute-start.10 = (bf16[2,32,1536]{2,1,0:T(8,128)(2,1)S(1)}, bf16[2,32,1536]{2,1,0:T(8,128)(2,1)S(1)}, u32[]{:S(2)}, u32[]{:S(2)}) collective-permute-start(bf16[2,32,1536]{2,1,0:T(8,128)(2,1)S(1)} %get-tuple-element.37), channel_id=1, source_target_pairs={{0,4},{1,5},{2,6},{3,7},{4,0},{5,1},{6,2},{7,3},{8,12},{9,13},{10,... | collective-permute-start | bytes 589832 | tf_op jit(solution)/shard_map/ppermute | solution.py:129
  140.7 9.2 %collective-permute-start.11 = (bf16[2,32,1536]{2,1,0:T(8,128)(2,1)S(1)}, bf16[2,32,1536]{2,1,0:T(8,128)(2,1)S(1)}, u32[]{:S(2)}, u32[]{:S(2)}) collective-permute-start(bf16[2,32,1536]{2,1,0:T(8,128)(2,1)S(1)} %get-tuple-element.38), channel_id=1, source_target_pairs={{0,5},{1,4},{2,7},{3,6},{4,1},{5,0},{6,3},{7,2},{8,13},{9,12},{10,... | collective-permute-start | bytes 589832 | tf_op jit(solution)/shard_map/ppermute | solution.py:129
  140.7 13.9 %collective-permute-start.12 = (bf16[2,32,1536]{2,1,0:T(8,128)(2,1)S(1)}, bf16[2,32,1536]{2,1,0:T(8,128)(2,1)S(1)}, u32[]{:S(2)}, u32[]{:S(2)}) collective-permute-start(bf16[2,32,1536]{2,1,0:T(8,128)(2,1)S(1)} %get-tuple-element.39), channel_id=1, source_target_pairs={{0,6},{1,7},{2,0},{3,1},{4,2},{5,3},{6,4},{7,5},{8,14},{9,15},{10,... | collective-permute-start | bytes 589832 | tf_op jit(solution)/shard_map/ppermute | solution.py:129
  142.1 14.5 %collective-permute-start.13 = (bf16[2,32,1536]{2,1,0:T(8,128)(2,1)S(1)}, bf16[2,32,1536]{2,1,0:T(8,128)(2,1)S(1)}, u32[]{:S(2)}, u32[]{:S(2)}) collective-permute-start(bf16[2,32,1536]{2,1,0:T(8,128)(2,1)S(1)} %get-tuple-element.40), channel_id=1, source_target_pairs={{0,7},{1,6},{2,1},{3,0},{4,3},{5,2},{6,5},{7,4},{8,15},{9,14},{10,... | collective-permute-start | bytes 589832 | tf_op jit(solution)/shard_map/ppermute | solution.py:129
  144.2 12.3 %collective-permute-start.7 = (bf16[2,32,1536]{2,1,0:T(8,128)(2,1)S(1)}, bf16[2,32,1536]{2,1,0:T(8,128)(2,1)S(1)}, u32[]{:S(2)}, u32[]{:S(2)}) collective-permute-start(bf16[2,32,1536]{2,1,0:T(8,128)(2,1)S(1)} %get-tuple-element.34), channel_id=1, source_target_pairs={{0,1},{1,0},{2,3},{3,2},{4,5},{5,4},{6,7},{7,6},{8,9},{9,8},{10,11... | collective-permute-start | bytes 589832 | tf_op jit(solution)/shard_map/ppermute | solution.py:129
  146.0 10.6 %collective-permute-start.8 = (bf16[2,32,1536]{2,1,0:T(8,128)(2,1)S(1)}, bf16[2,32,1536]{2,1,0:T(8,128)(2,1)S(1)}, u32[]{:S(2)}, u32[]{:S(2)}) collective-permute-start(bf16[2,32,1536]{2,1,0:T(8,128)(2,1)S(1)} %get-tuple-element.35), channel_id=1, source_target_pairs={{0,2},{1,3},{2,4},{3,5},{4,6},{5,7},{6,0},{7,1},{8,10},{9,11},{10,... | collective-permute-start | bytes 589832 | tf_op jit(solution)/shard_map/ppermute | solution.py:129
  149.9 7.6 %collective-permute-start.9 = (bf16[2,32,1536]{2,1,0:T(8,128)(2,1)S(1)}, bf16[2,32,1536]{2,1,0:T(8,128)(2,1)S(1)}, u32[]{:S(2)}, u32[]{:S(2)}) collective-permute-start(bf16[2,32,1536]{2,1,0:T(8,128)(2,1)S(1)} %get-tuple-element.36), channel_id=1, source_target_pairs={{0,3},{1,2},{2,5},{3,4},{4,7},{5,6},{6,1},{7,0},{8,11},{9,10},{10,... | collective-permute-start | bytes 589832 | tf_op jit(solution)/shard_map/ppermute | solution.py:129
Sparse Core Ops, SparseCore 0:
  9.5 96.0 all-gather.1
